TPU v7x, 512 devices: a whole 4x8x8 slice. The times are simulated.
512 devices in a mesh: col: 8 (over z_lo, core), row: 64 (over y, x, z_hi).
Axes of the slice: x: 4, y: 8, z: 8 (z_hi: 2, z_lo: 4; z = z_hi * 4 + z_lo), core: 2. Of those that a mesh axis runs over, the one named last changes fastest.
Arguments:
- trace: float32 [64, 64, 2048], P('col', None, 'row'), may hold values from -6 to 6
- step_coeff: float32 [64], P('col'), may hold values from -1 to 1
- pair_coeff: float32 [64], P('col'), may hold values from -1 to 1
- challenges: float32 [64], P('col'), may hold values from -0.25 to 0.25
Outputs:
- extension: float32 [2, 64, 64, 8192], P(None, 'col', None, 'row')
- quotient_values: float32 [2, 64, 8192], P(None, None, 'row')
- quotient_coeffs: float32 [2, 64, 8192], P(None, 'row')
All inputs are finite; a program needn't handle non-finite values.
Results may differ from a plain program's by a relative error of at most 0.0001.
Values sent between devices are 32-bit elements; how exact they have to be, the bound alone decides.
A program may use at most 64 MiB of HBM per device.

v0:
```python
import math

import jax
import jax.numpy as jnp
from jax import lax
from jax.sharding import PartitionSpec as P

HIGHEST = lax.Precision.HIGHEST


def from_behind(block, axis, distance):
    devices = range(lax.axis_size(axis))
    route = [((i - distance) % len(devices), i) for i in devices]
    return lax.ppermute(block, axis, route)


def phase_pair(integer_phase, modulus, orient):
    radians = integer_phase.astype(jnp.float32) * (orient * 2.0 * math.pi / modulus)
    return (jnp.cos(radians), jnp.sin(radians))


def phase_table(rows_count, cols_count, modulus, orient):
    row_index = lax.broadcasted_iota(jnp.int32, (rows_count, cols_count), 0)
    col_index = lax.broadcasted_iota(jnp.int32, (rows_count, cols_count), 1)
    return phase_pair(row_index * col_index % modulus, modulus, orient)


def complex_einsum(formula, real_part, imag_part, table_real, table_imag):
    real_out = jnp.einsum(formula, real_part, table_real, precision=HIGHEST) - jnp.einsum(
        formula, imag_part, table_imag, precision=HIGHEST
    )
    imag_out = jnp.einsum(formula, real_part, table_imag, precision=HIGHEST) + jnp.einsum(
        formula, imag_part, table_real, precision=HIGHEST
    )
    return (real_out, imag_out)


def rotate(real_part, imag_part, cosine, sine):
    return (real_part * cosine - imag_part * sine, real_part * sine + imag_part * cosine)


def split_length(length):
    chosen = 1
    for candidate in range(1, math.isqrt(length) + 1):
        if length % candidate == 0:
            chosen = candidate
    return chosen


def long_transform(real_part, imag_part, factor, orient):
    length = real_part.shape[-1]
    radix_outer = split_length(length)
    radix_inner = length // radix_outer
    leading = real_part.shape[:-1]
    widened = factor * radix_inner
    extended = factor * length
    real_grid = real_part.reshape(leading + (radix_inner, radix_outer))
    imag_grid = imag_part.reshape(leading + (radix_inner, radix_outer))
    first_cos, first_sin = phase_table(radix_inner, widened, widened, orient)
    real_grid, imag_grid = complex_einsum(
        "...ab,ac->...bc", real_grid, imag_grid, first_cos, first_sin
    )
    twist_cos, twist_sin = phase_table(radix_outer, widened, extended, orient)
    real_grid, imag_grid = rotate(real_grid, imag_grid, twist_cos, twist_sin)
    last_cos, last_sin = phase_table(radix_outer, radix_outer, radix_outer, orient)
    real_grid, imag_grid = complex_einsum(
        "...bc,bd->...dc", real_grid, imag_grid, last_cos, last_sin
    )
    return (real_grid.reshape(leading + (extended,)), imag_grid.reshape(leading + (extended,)))


def divide_vanishing(real_part, imag_part, point_index):
    zero_cos, zero_sin = phase_pair((2 * point_index + 1) % 8, 8, -1.0)
    zero_real = zero_cos - 1.0
    modulus_sq = zero_real * zero_real + zero_sin * zero_sin
    return (
        (real_part * zero_real + imag_part * zero_sin) / modulus_sq,
        (imag_part * zero_real - real_part * zero_sin) / modulus_sq,
    )


def shards(trace, step_coeff, pair_coeff, challenges):
    segments = lax.axis_size("row")
    row_place = lax.axis_index("row")
    columns = trace.shape[0]
    block_len = trace.shape[2]
    row_count = block_len * segments
    trace_len = row_count * segments
    coset_len = 4 * trace_len
    ext_block = 4 * block_len
    seg_cos, seg_sin = phase_table(segments, segments, segments, 1.0)
    head_real = jnp.einsum("cab,au->cub", trace, seg_cos, precision=HIGHEST)
    head_imag = jnp.einsum("cab,au->cub", trace, seg_sin, precision=HIGHEST)
    row_pos = row_place * block_len + lax.broadcasted_iota(jnp.int32, (segments, block_len), 1)
    seg_pos = lax.broadcasted_iota(jnp.int32, (segments, block_len), 0)
    turn_cos, turn_sin = phase_pair(row_pos * seg_pos % trace_len, trace_len, 1.0)
    head_real, head_imag = rotate(head_real, head_imag, turn_cos, turn_sin)
    stacked = jnp.stack([head_real, head_imag])
    arrived = lax.all_to_all(stacked, "row", split_axis=2, concat_axis=3, tiled=True)
    coef_real, coef_imag = long_transform(arrived[0], arrived[1], 1, 1.0)
    inverse_len = 1.0 / trace_len
    degree = row_place + segments * lax.broadcasted_iota(jnp.int32, (1, row_count), 1)
    shift_cos, shift_sin = phase_pair(degree, 2 * coset_len, -1.0)
    coef_real, coef_imag = rotate(
        coef_real * inverse_len, coef_imag * inverse_len, shift_cos, shift_sin
    )
    spread_real, spread_imag = long_transform(coef_real, coef_imag, 4, -1.0)
    point_index = lax.broadcasted_iota(jnp.int32, (1, 4 * row_count), 1)
    point_cos, point_sin = phase_pair(row_place * point_index % coset_len, coset_len, -1.0)
    spread_real, spread_imag = rotate(spread_real, spread_imag, point_cos, point_sin)
    spread = jnp.stack([spread_real, spread_imag])
    ext_cos, ext_sin = phase_table(segments, segments, segments, -1.0)
    arrived = lax.all_to_all(spread, "row", split_axis=3, concat_axis=2, tiled=True)
    real_out, imag_out = complex_einsum("cub,uv->cvb", arrived[0], arrived[1], ext_cos, ext_sin)
    extension = jnp.stack([real_out, imag_out])
    rim_next = from_behind(extension[:, :, :, :4], "row", -1)
    rim_next = jnp.where(row_place == segments - 1, jnp.roll(rim_next, -1, axis=2), rim_next)
    upcoming = jnp.concatenate([extension[:, :, :, 4:], rim_next], axis=3)
    partner = extension.reshape((2, columns // 2, 2) + extension.shape[2:])[:, :, ::-1].reshape(
        extension.shape
    )
    prod_real = extension[0] * partner[0] - extension[1] * partner[1]
    prod_imag = extension[0] * partner[1] + extension[1] * partner[0]
    weight_next = challenges[:, None, None]
    weight_step = (challenges * step_coeff)[:, None, None]
    weight_pair = (challenges * pair_coeff)[:, None, None]
    part_real = jnp.sum(
        weight_next * upcoming[0] - weight_step * extension[0] - weight_pair * prod_real, axis=0
    )
    part_imag = jnp.sum(
        weight_next * upcoming[1] - weight_step * extension[1] - weight_pair * prod_imag, axis=0
    )
    partial_value = jnp.stack([part_real, part_imag])
    quot_cos, quot_sin = phase_table(segments, segments, segments, 1.0)
    summed = lax.psum(partial_value, "col")
    point_index = row_place * ext_block + lax.broadcasted_iota(jnp.int32, (segments, ext_block), 1)
    value_real, value_imag = divide_vanishing(summed[0], summed[1], point_index)
    mixed_real, mixed_imag = complex_einsum("ab,au->ub", value_real, value_imag, quot_cos, quot_sin)
    class_index = lax.broadcasted_iota(jnp.int32, (segments, ext_block), 0)
    class_cos, class_sin = phase_pair(class_index * point_index % coset_len, coset_len, 1.0)
    mixed_real, mixed_imag = rotate(mixed_real, mixed_imag, class_cos, class_sin)
    lined_up = lax.all_to_all(
        jnp.stack([mixed_real, mixed_imag]), "row", split_axis=1, concat_axis=2, tiled=True
    )
    values = jnp.stack([value_real, value_imag])
    coef_real, coef_imag = long_transform(lined_up[0], lined_up[1], 1, 1.0)
    degree = row_place + segments * lax.broadcasted_iota(jnp.int32, (1, 4 * row_count), 1)
    shift_cos, shift_sin = phase_pair(degree, 2 * coset_len, 1.0)
    unitary_scale = 1.0 / math.sqrt(coset_len)
    coef_real, coef_imag = rotate(
        coef_real * unitary_scale, coef_imag * unitary_scale, shift_cos, shift_sin
    )
    quotient = jnp.stack([coef_real, coef_imag])
    return (extension, values, quotient)


def solution(mesh):
    placed = (P("col", None, "row"), P("col"), P("col"), P("col"))
    return jax.shard_map(
        shards,
        mesh=mesh,
        in_specs=placed,
        out_specs=(P(None, "col", None, "row"), P(None, None, "row"), P(None, "row", None)),
        check_vma=False,
    )
```

profile of v0, /device:TPU:1, one launch (start us, length us, event | category | flops | bytes accessed | tf_op | source)
XLA Modules:
  0.0 313.3 jit_solution(3704569130516163013)
XLA Ops:
  7.2 0.9 copy-done
  9.4 0.9 reshape.860
  10.3 19.7 %all-to-all-start = ((f32[64,1,512]{2,1,0:T(1,128)}), f32[64,1,512]{2,1,0:T(1,128)S(1)}, u32[]{:S(2)}, u32[]{:S(2)}) async-start(f32[64,1,512]{2,1,0:T(1,128)} %reshape.860), calls=%async_computation | async-start | bytes 262144 | tf_op jit(solution)/shard_map/all_to_all | solution.py:99
  30.6 13.1 %all-to-all-done = f32[64,1,512]{2,1,0:T(1,128)S(1)} async-done(((f32[64,1,512]{2,1,0:T(1,128)}), f32[64,1,512]{2,1,0:T(1,128)S(1)}, u32[]{:S(2)}, u32[]{:S(2)}) %all-to-all-start) | async-done | bytes 131104 | tf_op jit(solution)/shard_map/all_to_all | solution.py:99
  44.2 0.9 reduce.8
  53.7 12.5 %copy.83 = f32[2,8,1,8192]{1,2,0,3:T(1,128)} copy(f32[2,8,1,8192]{3,1,2,0:T(8,128)S(1)} %pad_maximum_fusion.1) | data formatting | bytes 1048576 | tf_op jit(solution)/shard_map/stack | solution.py:111
  66.2 30.8 %reduce.9 = f32[8192,2,8]{2,1,0:T(2,128)} reduce(f32[8192,2,1,8]{3,2,1,0:T(1,128)} %bitcast.225, f32[]{:T(128)} %broadcast.967), dimensions={2}, to_apply=%bitcast.205.reduce_sub_computation | reduce | bytes 1048580
  97.0 13.6 %reshape.862 = f32[64,1,2048]{2,1,0:T(1,128)} reshape(f32[8192,2,8]{2,1,0:T(2,128)} %reduce.9) | data formatting | bytes 1048576
  110.6 4.6 %all-to-all-start.1 = ((f32[64,1,2048]{2,1,0:T(1,128)}), f32[64,1,2048]{2,1,0:T(1,128)S(1)}, u32[]{:S(2)}, u32[]{:S(2)}) async-start(f32[64,1,2048]{2,1,0:T(1,128)} %reshape.862), calls=%async_computation.1 | async-start | bytes 1048576 | tf_op jit(solution)/shard_map/all_to_all | solution.py:113
  115.4 17.9 %all-to-all-done.1 = f32[64,1,2048]{2,1,0:T(1,128)S(1)} async-done(((f32[64,1,2048]{2,1,0:T(1,128)}), f32[64,1,2048]{2,1,0:T(1,128)S(1)}, u32[]{:S(2)}, u32[]{:S(2)}) %all-to-all-start.1) | async-done | bytes 524320 | tf_op jit(solution)/shard_map/all_to_all | solution.py:113
  133.3 1.9 reduce.10
  135.2 15.7 %reshape.863 = f32[8192,2,1,8]{3,2,1,0:T(1,128)} reshape(f32[64,2048]{1,0:T(8,128)S(1)} %reduce.10) | data formatting | bytes 1048576
  150.9 7.3 %fusion.331 = (f32[1,8,1,8192]{1,2,0,3:T(1,128)}, f32[1,8,1,8192]{1,2,0,3:T(1,128)}) fusion(f32[2,8,1,8192]{1,2,0,3:T(1,128)} %bitcast.226), kind=kLoop, calls=%fused_computation.423 | loop fusion | bytes 1048576 | tf_op jit(solution)/shard_map/slice | solution.py:114
  158.2 2.8 copy.101
  162.0 2.8 copy.102
  165.9 4.0 %collective-permute-start = (f32[2,8,64,4]{3,2,1,0:T(8,128)S(1)}, f32[2,8,64,4]{3,2,1,0:T(8,128)S(1)}, u32[]{:S(2)}, u32[]{:S(2)}) collective-permute-start(f32[2,8,64,4]{3,2,1,0:T(8,128)S(1)} %fusion.7), channel_id=1, source_target_pairs={{1,0},{2,1},{3,2},{4,3},{5,4},{6,5},{7,6},{8,7},{9,8},{10,9},{11,1... | collective-permute-start | bytes 49160 | tf_op jit(solution)/shard_map/ppermute | solution.py:14
  170.2 13.2 %collective-permute-done = f32[2,8,64,4]{3,2,1,0:T(8,128)S(1)} collective-permute-done((f32[2,8,64,4]{3,2,1,0:T(8,128)S(1)}, f32[2,8,64,4]{3,2,1,0:T(8,128)S(1)}, u32[]{:S(2)}, u32[]{:S(2)}) %collective-permute-start) | collective-permute-done | bytes 16416 | tf_op jit(solution)/shard_map/ppermute | solution.py:14
  185.3 83.3 %all-reduce.2.cloned.1.call-done = f32[2,64,128]{2,1,0:T(8,128)} async-done(((f32[2,64,128]{2,1,0:T(8,128)}), f32[2,64,128]{2,1,0:T(8,128)}) %all-reduce.2.cloned.1.call-update) | async-done | bytes 65552 | tf_op jit(solution)/shard_map/psum | solution.py:135
  270.0 1.1 convolution_add_fusion.7
  271.1 1.1 subtract_bitcast_fusion.1
  273.0 14.4 %all-to-all-start.2 = ((f32[2,64,128]{2,0,1:T(2,128)}), f32[2,64,128]{2,0,1:T(2,128)S(1)}, u32[]{:S(2)}, u32[]{:S(2)}) async-start(f32[2,64,128]{2,0,1:T(2,128)} %copy.86), calls=%async_computation.2 | async-start | bytes 131072 | tf_op jit(solution)/shard_map/all_to_all | solution.py:142
  287.4 0.8 fusion.90
  288.9 12.0 %all-to-all-done.2 = f32[2,64,128]{2,0,1:T(2,128)S(1)} async-done(((f32[2,64,128]{2,0,1:T(2,128)}), f32[2,64,128]{2,0,1:T(2,128)S(1)}, u32[]{:S(2)}, u32[]{:S(2)}) %all-to-all-start.2) | async-done | bytes 65568 | tf_op jit(solution)/shard_map/all_to_all | solution.py:142
  304.7 1.1 multiply_subtract_fusion.8
  (83 shorter events, 22.2 us)
Async XLA Ops:
  7.2 0.9 copy-start
  10.3 33.4 %all-to-all-start = ((f32[64,1,512]{2,1,0:T(1,128)}), f32[64,1,512]{2,1,0:T(1,128)S(1)}, u32[]{:S(2)}, u32[]{:S(2)}) async-start(f32[64,1,512]{2,1,0:T(1,128)} %reshape.860), calls=%async_computation | async-start | bytes 262144 | tf_op jit(solution)/shard_map/all_to_all | solution.py:99
  97.0 18.4 %copy-start.1 = (f32[8]{0:T(128)S(1)}, f32[8]{0:T(128)}, u32[]{:S(2)}) copy-start(f32[8]{0:T(128)} %param.7) | copy-start | bytes 100
  97.0 18.4 %copy-start.2 = (f32[8]{0:T(128)S(1)}, f32[8]{0:T(128)}, u32[]{:S(2)}) copy-start(f32[8]{0:T(128)} %param.5) | copy-start | bytes 100
  97.0 18.4 %copy-start.3 = (f32[8]{0:T(128)S(1)}, f32[8]{0:T(128)}, u32[]{:S(2)}) copy-start(f32[8]{0:T(128)} %param.6) | copy-start | bytes 100
  110.6 22.7 %all-to-all-start.1 = ((f32[64,1,2048]{2,1,0:T(1,128)}), f32[64,1,2048]{2,1,0:T(1,128)S(1)}, u32[]{:S(2)}, u32[]{:S(2)}) async-start(f32[64,1,2048]{2,1,0:T(1,128)} %reshape.862), calls=%async_computation.1 | async-start | bytes 1048576 | tf_op jit(solution)/shard_map/all_to_all | solution.py:113
  115.3 153.3 %all-reduce.2.cloned.1.call-start = ((), (), s32[]{:S(2)}) async-start(), calls=%async_computation.3 | async-start | bytes 131072 | tf_op jit(solution)/shard_map/psum | solution.py:135
  165.9 17.4 %collective-permute-start = (f32[2,8,64,4]{3,2,1,0:T(8,128)S(1)}, f32[2,8,64,4]{3,2,1,0:T(8,128)S(1)}, u32[]{:S(2)}, u32[]{:S(2)}) collective-permute-start(f32[2,8,64,4]{3,2,1,0:T(8,128)S(1)} %fusion.7), channel_id=1, source_target_pairs={{1,0},{2,1},{3,2},{4,3},{5,4},{6,5},{7,6},{8,7},{9,8},{10,9},{11,1... | collective-permute-start | bytes 49160 | tf_op jit(solution)/shard_map/ppermute | solution.py:14
  273.0 27.9 %all-to-all-start.2 = ((f32[2,64,128]{2,0,1:T(2,128)}), f32[2,64,128]{2,0,1:T(2,128)S(1)}, u32[]{:S(2)}, u32[]{:S(2)}) async-start(f32[2,64,128]{2,0,1:T(2,128)} %copy.86), calls=%async_computation.2 | async-start | bytes 131072 | tf_op jit(solution)/shard_map/all_to_all | solution.py:142
Sparse Core Ops, SparseCore 0:
  184.6 83.9 all-reduce.1
where the time goes:
time: 314 us; the launch traced here: 313 us
  waiting for transfers between devices  139 us (44%)
  local copies, waits for them, and re-layouts  59.2 us (19%)
  starting transfers between devices  42.8 us (14%)
  other arithmetic  40.7 us (13%)
  matrix products  16.6 us (5%)
  between operations  14.6 us (5%)
    psum x1, waiting for transfers between devices, shards(): summed = lax.psum(partial_value, 'col')  83.3 us
    unnamed x14, local copies, waits for them, and re-layouts  31.6 us
    unnamed x1, other arithmetic  30.8 us
    all_to_all x1, starting transfers between devices, shards(): lax.all_to_all(stacked, 'row', split_axis=2, concat_axis=3, tiled=True)  19.7 us
    all_to_all x1, waiting for transfers between devices, shards(): lax.all_to_all(spread, 'row', split_axis=3, concat_axis=2, tiled=True)  17.9 us
    all_to_all x1, starting transfers between devices, shards(): lax.all_to_all(jnp.stack([mixed_real, mixed_imag]), 'row', split_axis=1,...  14.4 us
    ppermute x1, waiting for transfers between devices, from_behind(): return lax.ppermute(block, axis, route)  13.2 us
    all_to_all x1, waiting for transfers between devices, shards(): lax.all_to_all(stacked, 'row', split_axis=2, concat_axis=3, tiled=True)  13.1 us
  transfers between devices with their start and end apart: 5, of which 5 were waited for; matrix products, arithmetic and copies ran while one was open for 1% of the time, Pallas kernels for 0%

commit v1 on v0

v1 whole, which is shorter than its diff:
```python
import math

import jax
import jax.numpy as jnp
import numpy as np
from jax import lax
from jax.experimental import pallas as pl
from jax.experimental.pallas import tpu as pltpu
from jax.sharding import PartitionSpec as P

SEG = 64
COLS = 8
PAIRS = 4
RUN = 32
LANES = 128
TRACE_LEN = SEG * SEG * RUN
COSET_LEN = 4 * TRACE_LEN
MESH = pl.DeviceIdType.MESH
F32 = jnp.float32
BF16 = jnp.bfloat16


def halves(matrix):
    high = matrix.astype(BF16)
    low = (matrix - high.astype(np.float64)).astype(BF16)
    return np.stack([high, low])


def complex_rows(angle):
    return np.stack([np.cos(angle), np.sin(angle)])


def real_form(angle, out_order, in_order):
    cosine, sine = np.cos(angle), np.sin(angle)
    grid = np.stack([np.stack([cosine, -sine]), np.stack([sine, cosine])])
    places = {"co": (0, 2), "oc": (2, 0), "ci": (1, 3), "ic": (3, 1)}
    rows, cols = angle.shape
    return grid.transpose(places[out_order] + places[in_order]).reshape(2 * rows, 2 * cols)


def build_tables():
    tau = 2.0 * np.pi
    seg = np.arange(SEG)
    run = np.arange(RUN)
    first = real_form(tau * np.outer(seg, seg) / SEG, "oc", "ci")
    middle = []
    vectors = []
    lane = np.arange(LANES)
    offset = lane // 4 + (2 * (lane % 4) + 1) / 8.0
    rim = RUN + (2 * (lane % 4) + 1) / 8.0
    rim_here = (lane >= LANES - 16).astype(np.float64)
    beta = np.tile(run, PAIRS)
    for u in range(SEG):
        angle = tau * np.outer(SEG * seg + u, seg) / (SEG * SEG)
        matrix = real_form(angle, "co", "ic")
        middle.append(np.stack([halves(matrix), halves(matrix.T)]))
        vectors.append(
            np.concatenate(
                [
                    complex_rows(tau * beta * u / TRACE_LEN),
                    complex_rows(-tau * offset * u / TRACE_LEN),
                    complex_rows(-tau * rim * u / TRACE_LEN),
                    complex_rows(tau * (2 * lane + 1) * u / (2 * COSET_LEN)),
                ]
            )
        )
    twist_in = complex_rows(tau * beta * (64 * seg[:, None] - 2048) / TRACE_LEN)
    twist_out = complex_rows(-tau * offset * (64 * seg[:, None] - 2048) / TRACE_LEN) / TRACE_LEN
    twist_rim = (
        complex_rows(-tau * rim * (64 * seg[:, None] - 2048) / TRACE_LEN) / TRACE_LEN * rim_here
    )
    twist_quot = complex_rows(
        tau * (2 * lane + 1) * (64 * seg[:, None]) / (2 * COSET_LEN)
    ) / math.sqrt(COSET_LEN)
    twists = np.concatenate([twist_in, twist_out, twist_rim, twist_quot])
    spread = np.zeros((PAIRS, RUN, 5, LANES))
    mean = np.zeros((PAIRS, RUN, LANES))
    for j in range(PAIRS):
        spread[j, :, j, :] = 1.0 / np.sin(np.pi * (offset[None, :] - run[:, None]) / RUN)
        own = (lane >= LANES - 16) & ((lane - (LANES - 16)) // 4 == j)
        spread[j, :, 4, :] = own / np.sin(np.pi * (rim[None, :] - run[:, None]) / RUN)
        mean[j, :, j] = 1.0 / TRACE_LEN
    spread = spread.reshape(LANES, 5 * LANES)
    half = np.arange(SEG)
    order = np.concatenate([2 * half, 2 * half + 1])
    last = real_form(tau * np.outer(order, 2 * lane + 1) / 256.0, "co", "ci")
    shape = (2 * (lane % 4) + 1) / 8.0
    gain = np.exp(-1j * np.pi * shape) * np.sin(np.pi * shape)
    vanish = 1.0 / (np.exp(-1j * np.pi * (2 * (lane % 4) + 1) / 4.0) - 1.0)
    scales = []
    for value in (gain, gain * vanish, gain * gain * vanish):
        scales += [value.real, value.imag]
    scales += [np.zeros(LANES)] * 2
    return {
        "vectors": np.stack(vectors).astype(np.float32),
        "middle": np.stack(middle),
        "first": np.stack([halves(first), halves(first.T)]),
        "twists": twists.astype(np.float32),
        "spread": halves(spread),
        "mean": mean.reshape(LANES, LANES).astype(BF16),
        "last": halves(last),
        "scales": np.stack(scales).astype(np.float32),
    }


def parts_of(value):
    high = value.astype(BF16)
    low = (value - high.astype(F32)).astype(BF16)
    return high, low


def left_dot(table, value):
    high, low = parts_of(value)
    left = jnp.concatenate([table[0], table[0], table[1]], axis=1)
    right = jnp.concatenate([high, low, high], axis=0)
    return jnp.dot(left, right, preferred_element_type=F32)


def right_dot(value, table):
    high, low = parts_of(value)
    left = jnp.concatenate([high, low, high], axis=1)
    right = jnp.concatenate([table[0], table[0], table[1]], axis=0)
    return jnp.dot(left, right, preferred_element_type=F32)


def turn(real, imag, cosine, sine):
    return real * cosine - imag * sine, real * sine + imag * cosine


def kernel(
    trace_hbm, step_ref, pair_ref, chal_ref,
    vectors_hbm, middle_hbm, first_hbm, twists_hbm, spread_hbm, mean_hbm, last_hbm, scales_hbm,
    ext_hbm, val_hbm, quot_hbm,
    trace, vectors, middle, first, twists, spread, mean, last, scales,
    ext, val, quot,
    send1, recv1, send2, recv2, send3, recv3, send4, recv4, send5, recv5,
    load_sems, store_sems, send_sems, recv_sems,
):
    me = lax.axis_index("row")
    col = lax.axis_index("col")

    barrier = pltpu.get_barrier_semaphore()

    def greet_row(k, carry):
        pl.semaphore_signal(
            barrier, inc=1, device_id={"row": lax.rem(me + k, SEG)}, device_id_type=MESH
        )
        return carry

    def greet_col(k, carry):
        pl.semaphore_signal(
            barrier, inc=1, device_id={"col": lax.rem(col + k, COLS)}, device_id_type=MESH
        )
        return carry

    loads = [
        pltpu.make_async_copy(src, dst, load_sems.at[i])
        for i, (src, dst) in enumerate(
            [
                (trace_hbm, trace),
                (first_hbm, first),
                (vectors_hbm.at[me], vectors),
                (middle_hbm.at[me], middle),
                (twists_hbm, twists),
                (spread_hbm, spread),
                (mean_hbm, mean),
                (scales_hbm, scales),
                (last_hbm, last),
            ]
        )
    ]
    for load in loads:
        load.start()
    lax.fori_loop(1, SEG, greet_row, 0)
    lax.fori_loop(1, COLS, greet_col, 0)

    loads[0].wait()
    loads[1].wait()
    grid = jnp.concatenate(
        [
            jnp.concatenate([trace[2 * j + c] for j in range(PAIRS)], axis=1)
            for c in range(2)
        ],
        axis=0,
    )
    head = left_dot(first[0], grid)
    send1[...] = head.reshape(SEG, 2, LANES)
    recv1[me] = send1[me]
    pl.semaphore_wait(barrier, SEG - 1 + COLS - 1)

    def post1(k, carry):
        peer = lax.rem(me + k, SEG)
        pltpu.make_async_remote_copy(
            src_ref=send1.at[peer], dst_ref=recv1.at[me],
            send_sem=send_sems.at[0], recv_sem=recv_sems.at[0],
            device_id={"row": peer}, device_id_type=MESH,
        ).start()
        return carry

    lax.fori_loop(1, SEG, post1, 0)

    for load in loads[2:]:
        load.wait()
    head_high, head_low = parts_of(head[:8])
    sums = jnp.dot(head_high, mean[...], preferred_element_type=F32) + jnp.dot(
        head_low, mean[...], preferred_element_type=F32
    )
    parity = lax.broadcasted_iota(jnp.int32, (LANES, LANES), 0) % 2
    sums = jnp.where(parity == 0, sums[0:1], sums[1:2])

    def table(index, row):
        base = twists[2 * index], twists[2 * index + 1]
        return turn(*base, vectors[2 * row : 2 * row + 1], vectors[2 * row + 1 : 2 * row + 2])

    in_cos, in_sin = table(0, 0)
    out_cos, out_sin = table(1, 1)
    rim_cos, rim_sin = table(2, 2)

    pltpu.make_async_copy(
        recv1.at[pl.ds(0, SEG - 1)], recv1.at[pl.ds(0, SEG - 1)], recv_sems.at[0]
    ).wait()

    mixed = left_dot(middle[0], recv1[...].reshape(LANES, LANES))
    real, imag = turn(mixed[:SEG], mixed[SEG:], in_cos, in_sin)
    wide = right_dot(jnp.concatenate([real, imag], axis=0), spread)
    pieces = []
    for j in range(5):
        cosine, sine = (out_cos, out_sin) if j < 4 else (rim_cos, rim_sin)
        part = wide[:, LANES * j : LANES * (j + 1)]
        real, imag = turn(part[:SEG], part[SEG:], cosine, sine)
        pieces.append(jnp.concatenate([real, imag], axis=0))
    back = left_dot(middle[1], jnp.concatenate(pieces, axis=1))
    for j in range(5):
        part = back[:, LANES * j : LANES * (j + 1)]
        if j == 4:
            part = part + sums
        send2[j] = part.reshape(SEG, 2, LANES)
    for j in range(5):
        recv2[j, me] = send2[j, me]

    def post2(k, carry):
        peer = lax.rem(me + k, SEG)
        pltpu.make_async_remote_copy(
            src_ref=send2.at[:, peer], dst_ref=recv2.at[:, me],
            send_sem=send_sems.at[1], recv_sem=recv_sems.at[1],
            device_id={"row": peer}, device_id_type=MESH,
        ).start()
        return carry

    lax.fori_loop(1, SEG, post2, 0)
    quot_cos, quot_sin = table(3, 3)
    pltpu.make_async_copy(
        recv2.at[:, pl.ds(0, SEG - 1)], recv2.at[:, pl.ds(0, SEG - 1)], recv_sems.at[1]
    ).wait()

    arrived = jnp.concatenate([recv2[j].reshape(LANES, LANES) for j in range(5)], axis=1)
    field = left_dot(first[1], arrived)

    def scale(row):
        return scales[2 * row : 2 * row + 1], scales[2 * row + 1 : 2 * row + 2]

    rim_part = field[:, 4 * LANES :]
    lane = lax.broadcasted_iota(jnp.int32, (SEG, LANES), 1)
    gain_real, gain_imag = scale(0)
    ahead = jnp.zeros((SEG, LANES), F32)
    own = jnp.zeros((SEG, LANES), F32)
    product = jnp.zeros((SEG, LANES), F32)
    cross = jnp.zeros((SEG, LANES), F32)
    rim_weight = [jnp.zeros((SEG, LANES), F32)] * 2
    level_ahead = jnp.zeros((1, 1), F32)
    level_own = jnp.zeros((1, 1), F32)
    level_product = jnp.zeros((1, 1), F32)
    for j in range(PAIRS):
        mean_c = rim_part[0:1, j : j + 1]
        mean_d = rim_part[SEG : SEG + 1, j : j + 1]
        chal_c, chal_d = chal_ref[2 * j], chal_ref[2 * j + 1]
        step_c, step_d = chal_c * step_ref[2 * j], chal_d * step_ref[2 * j + 1]
        weight = chal_c * pair_ref[2 * j] + chal_d * pair_ref[2 * j + 1]
        raw_c = field[:SEG, LANES * j : LANES * (j + 1)]
        raw_d = field[SEG:, LANES * j : LANES * (j + 1)]
        real_c = raw_c + mean_d
        real_d = raw_d - mean_c
        ext[0, 2 * j] = gain_real * real_c - gain_imag * mean_c
        ext[1, 2 * j] = gain_imag * real_c + gain_real * mean_c
        ext[0, 2 * j + 1] = gain_real * real_d - gain_imag * mean_d
        ext[1, 2 * j + 1] = gain_imag * real_d + gain_real * mean_d
        ahead += chal_c * raw_c + chal_d * raw_d
        own += step_c * real_c + step_d * real_d
        product += weight * (real_c * real_d)
        cross += weight * (real_c * mean_d + real_d * mean_c)
        group = (lane >= LANES - 16 + 4 * j) & (lane < LANES - 12 + 4 * j)
        rim_weight = [
            jnp.where(group, chal_c, rim_weight[0]),
            jnp.where(group, chal_d, rim_weight[1]),
        ]
        level_ahead += chal_c * mean_d - chal_d * mean_c
        level_own += (chal_c - step_c) * mean_c + (chal_d - step_d) * mean_d
        level_product += weight * (mean_c * mean_d)
    ext_copy = pltpu.make_async_copy(ext, ext_hbm, store_sems.at[0])
    ext_copy.start()
    rim_sum = rim_part[:SEG] * rim_weight[0] + rim_part[SEG:] * rim_weight[1]
    rim_sum = rim_sum + pltpu.roll(rim_sum, 4, 1)
    rim_sum = rim_sum + pltpu.roll(rim_sum, 8, 1)
    ahead = jnp.where(lane < LANES - 4, pltpu.roll(ahead, LANES - 4, 1), rim_sum)
    line_real = ahead + level_ahead - own
    line_imag = level_own
    square_real = product - level_product
    square_imag = cross
    line_scale, square_scale = scale(1), scale(2)
    value_real = (
        line_scale[0] * line_real
        - line_scale[1] * line_imag
        - square_scale[0] * square_real
        + square_scale[1] * square_imag
    )
    value_imag = (
        line_scale[0] * line_imag
        + line_scale[1] * line_real
        - square_scale[0] * square_imag
        - square_scale[1] * square_real
    )
    mixed = left_dot(first[0], jnp.concatenate([value_real, value_imag], axis=0))
    for i in range(COLS):
        send3[i, 0:16] = mixed[16 * i : 16 * (i + 1)]
        send3[i, 16:24] = value_real[8 * i : 8 * (i + 1)]
        send3[i, 24:32] = value_imag[8 * i : 8 * (i + 1)]

    def post3(k, carry):
        peer = lax.rem(col + k, COLS)
        pltpu.make_async_remote_copy(
            src_ref=send3.at[peer], dst_ref=recv3.at[col],
            send_sem=send_sems.at[2], recv_sem=recv_sems.at[2],
            device_id={"col": peer}, device_id_type=MESH,
        ).start()
        return carry

    lax.fori_loop(1, COLS, post3, 0)
    recv3[col] = send3[col]
    pltpu.make_async_copy(
        recv3.at[pl.ds(0, COLS - 1)], recv3.at[pl.ds(0, COLS - 1)], recv_sems.at[2]
    ).wait()
    total = recv3[0]
    for i in range(1, COLS):
        total = total + recv3[i]
    send4[...] = total[:16].reshape(8, 2, LANES)
    send5[...] = total[16:]

    here = lax.div(me, COLS) == col

    def post4(k, carry):
        line = lax.rem(lax.div(k, COLS) + me, COLS)
        across = lax.rem(k + col, COLS)
        target = col * COLS + line
        alone = (target == me) & (across == col)

        @pl.when(jnp.logical_not(alone))
        def _():
            pltpu.make_async_remote_copy(
                src_ref=send4.at[line], dst_ref=recv4.at[me],
                send_sem=send_sems.at[3], recv_sem=recv_sems.at[3],
                device_id={"col": across, "row": target}, device_id_type=MESH,
            ).start()

        @pl.when(alone)
        def _():
            pltpu.make_async_copy(send4.at[line], recv4.at[me], recv_sems.at[3]).start()

        return carry

    lax.fori_loop(0, SEG, post4, 0)

    def post5(k, carry):
        pltpu.make_async_remote_copy(
            src_ref=send5, dst_ref=recv5.at[col],
            send_sem=send_sems.at[4], recv_sem=recv_sems.at[4],
            device_id={"col": lax.rem(col + k, COLS)}, device_id_type=MESH,
        ).start()
        return carry

    lax.fori_loop(1, COLS, post5, 0)
    recv5[col] = send5[...]

    pltpu.make_async_copy(recv4, recv4, recv_sems.at[3]).wait()
    mixed = left_dot(middle[0], recv4[...].reshape(LANES, LANES))
    real, imag = turn(mixed[:SEG], mixed[SEG:], quot_cos, quot_sin)
    both = jnp.concatenate([real, imag], axis=1)
    both = jnp.concatenate([both, both], axis=0)
    high, low = parts_of(both)
    result = lax.dot_general(
        jnp.concatenate([last[0], last[0], last[1]], axis=1),
        jnp.concatenate([high, low, high], axis=1),
        (((1,), (1,)), ((), ())),
        preferred_element_type=F32,
    )
    for c in range(2):
        even = result[LANES * c : LANES * c + SEG]
        odd = result[LANES * c + SEG : LANES * (c + 1)]
        quot[c] = jnp.where(lane < SEG, even, odd)
    quot_copy = pltpu.make_async_copy(quot, quot_hbm, store_sems.at[1])
    quot_copy.start()

    pltpu.make_async_copy(
        recv5.at[pl.ds(0, COLS - 1)], recv5.at[pl.ds(0, COLS - 1)], recv_sems.at[4]
    ).wait()
    for i in range(COLS):
        val[0, 8 * i : 8 * (i + 1)] = recv5[i, 0:8]
        val[1, 8 * i : 8 * (i + 1)] = recv5[i, 8:16]
    val_copy = pltpu.make_async_copy(val, val_hbm, store_sems.at[2])
    val_copy.start()

    pltpu.make_async_copy(
        send1.at[pl.ds(0, SEG - 1)], send1.at[pl.ds(0, SEG - 1)], send_sems.at[0]
    ).wait()
    pltpu.make_async_copy(
        send2.at[:, pl.ds(0, SEG - 1)], send2.at[:, pl.ds(0, SEG - 1)], send_sems.at[1]
    ).wait()
    pltpu.make_async_copy(
        send3.at[pl.ds(0, COLS - 1)], send3.at[pl.ds(0, COLS - 1)], send_sems.at[2]
    ).wait()

    @pl.when(here)
    def _():
        pltpu.make_async_copy(
            recv4.at[pl.ds(0, SEG - 1)], recv4.at[pl.ds(0, SEG - 1)], send_sems.at[3]
        ).wait()

    @pl.when(jnp.logical_not(here))
    def _():
        pltpu.make_async_copy(recv4, recv4, send_sems.at[3]).wait()

    pltpu.make_async_copy(
        recv5.at[pl.ds(0, COLS - 1)], recv5.at[pl.ds(0, COLS - 1)], send_sems.at[4]
    ).wait()
    ext_copy.wait()
    quot_copy.wait()
    val_copy.wait()


def shards(trace, step_coeff, pair_coeff, challenges):
    tables = build_tables()
    names = ["vectors", "middle", "first", "twists", "spread", "mean", "last", "scales"]
    constants = [jnp.asarray(tables[name]) for name in names]
    vmem = pltpu.VMEM
    anywhere = pl.BlockSpec(memory_space=pl.ANY)
    scalar = pl.BlockSpec(memory_space=pltpu.SMEM)
    outs = (
        jax.ShapeDtypeStruct((2, COLS, SEG, LANES), F32),
        jax.ShapeDtypeStruct((2, SEG, LANES), F32),
        jax.ShapeDtypeStruct((2, SEG, LANES), F32),
    )
    tables_scratch = [
        vmem(c.shape[1:] if n in ("vectors", "middle") else c.shape, c.dtype)
        for n, c in zip(names, constants, strict=True)
    ]
    extension, values, quotient = pl.pallas_call(
        kernel,
        out_shape=outs,
        in_specs=[anywhere, scalar, scalar, scalar] + [anywhere] * len(constants),
        out_specs=(anywhere,) * 3,
        scratch_shapes=[
            vmem(trace.shape, F32),
            *tables_scratch,
            *[vmem(o.shape, F32) for o in outs],
            vmem((SEG, 2, LANES), F32),
            vmem((SEG, 2, LANES), F32),
            vmem((5, SEG, 2, LANES), F32),
            vmem((5, SEG, 2, LANES), F32),
            vmem((COLS, 32, LANES), F32),
            vmem((COLS, 32, LANES), F32),
            vmem((8, 2, LANES), F32),
            vmem((SEG, 2, LANES), F32),
            vmem((16, LANES), F32),
            vmem((COLS, 16, LANES), F32),
            pltpu.SemaphoreType.DMA((9,)),
            pltpu.SemaphoreType.DMA((3,)),
            pltpu.SemaphoreType.DMA((5,)),
            pltpu.SemaphoreType.DMA((5,)),
        ],
        compiler_params=pltpu.CompilerParams(
            collective_id=0, has_side_effects=True, vmem_limit_bytes=32 * 1024 * 1024
        ),
    )(trace, step_coeff, pair_coeff, challenges, *constants)
    return extension, values, quotient.reshape(2, 1, SEG * LANES)


def solution(mesh):
    placed = (P("col", None, "row"), P("col"), P("col"), P("col"))
    return jax.shard_map(
        shards,
        mesh=mesh,
        in_specs=placed,
        out_specs=(P(None, "col", None, "row"), P(None, None, "row"), P(None, "row", None)),
        check_vma=False,
    )
```

time: 314 us -> 71 us (0.23)
  waiting for transfers between devices: 139 us -> 0 us
  Pallas kernels: 0 us -> 55.3 us
  local copies, waits for them, and re-layouts: 59.2 us -> 14.6 us
  starting transfers between devices: 42.8 us -> 0 us
  other arithmetic: 40.7 us -> 0 us
  matrix products: 16.6 us -> 0 us
  between operations: 14.6 us -> 0.67 us
    psum x1 -> x0, waiting for transfers between devices: 83.3 us -> none  [shards(): summed = lax.psum(partial_value, 'col')]
    pallas_call x0 -> x1, Pallas kernels: none -> 55.3 us  [shards(): pl.pallas_call(kernel, out_shape=outs, in_specs=[anywhere, scalar, scalar...]
    all_to_all x3 -> x0, waiting for transfers between devices: 43 us -> none  [the longest x1 17.9 us: shards(): lax.all_to_all(spread, 'row', split_axis=3, concat_axis=2, tiled=True)]
    all_to_all x3 -> x0, starting transfers between devices: 38.8 us -> none  [the longest x1 19.7 us: shards(): lax.all_to_all(stacked, 'row', split_axis=2, concat_axis=3, tiled=True)]
    unnamed x1 -> x0, other arithmetic: 30.8 us -> none
    unnamed x14 -> x26, local copies, waits for them, and re-layouts: 31.6 us -> 14.6 us
    dot_general x32 -> x0, matrix products: 15.8 us -> none  [the longest x8 4.41 us: complex_einsum(): jnp.einsum(formula, imag_part, table_imag, precision=HIGHEST)]
    another operation x5 -> x0, local copies, waits for them, and re-layouts: 13.6 us -> none  [the longest x1 12.5 us: shards(): spread = jnp.stack([spread_real, spread_imag])]
  transfers between devices with their start and end apart: 5 -> 0, of which waited for: 5 -> 0; matrix products, arithmetic and copies ran while one was open for 1% -> 0% of each run, Pallas kernels for 0% -> 0%
where the time goes in v1:
time: 71 us; the launch traced here: 70.5 us
  Pallas kernels  55.3 us (78%)
  local copies, waits for them, and re-layouts  14.6 us (21%)
    pallas_call x1, Pallas kernels, shards(): pl.pallas_call(kernel, out_shape=outs, in_specs=[anywhere, scalar, scalar...  55.3 us
    unnamed x26, local copies, waits for them, and re-layouts  14.6 us

profile of v1, /device:TPU:1, one launch (start us, length us, event | category | flops | bytes accessed | tf_op | source)
XLA Modules:
  0.0 70.5 jit_solution(14296204304774061875)
XLA Ops:
  0.6 1.0 %copy.15.trace_hbm = f32[8,64,32]{2,1,0:T(8,128)S(1)} copy(f32[8,64,32]{1,2,0:T(8,128)} %param.12) | data formatting | bytes 131072 | tf_op args[0]
  1.7 0.0 copy-start
  1.7 3.4 %copy-done = bf16[64,2,2,128,128]{4,3,2,1,0:T(8,128)(2,1)S(1)} copy-done((bf16[64,2,2,128,128]{4,3,2,1,0:T(8,128)(2,1)S(1)}, bf16[64,2,2,128,128]{4,3,2,1,0:T(8,128)(2,1)}, u32[]{:S(2)}) %copy-start) | copy-done | bytes 8388632
  5.1 0.0 copy-start.1
  5.1 1.0 %copy-done.1 = bf16[2,128,640]{2,1,0:T(8,128)(2,1)S(1)} copy-done((bf16[2,128,640]{2,1,0:T(8,128)(2,1)S(1)}, bf16[2,128,640]{2,1,0:T(8,128)(2,1)}, u32[]{:S(2)}) %copy-start.1) | copy-done | bytes 327704
  6.0 0.0 copy-start.2
  6.0 0.9 %copy-done.2 = bf16[2,256,256]{2,1,0:T(8,128)(2,1)S(1)} copy-done((bf16[2,256,256]{2,1,0:T(8,128)(2,1)S(1)}, bf16[2,256,256]{2,1,0:T(8,128)(2,1)}, u32[]{:S(2)}) %copy-start.2) | copy-done | bytes 262168
  7.0 0.0 copy-start.3
  7.0 0.9 %copy-done.3 = f32[8,64,128]{2,1,0:T(8,128)S(1)} copy-done((f32[8,64,128]{2,1,0:T(8,128)S(1)}, f32[8,64,128]{2,1,0:T(8,128)}, u32[]{:S(2)}) %copy-start.3) | copy-done | bytes 262168
  7.9 0.9 %copy-done.4 = f32[64,8,128]{2,1,0:T(8,128)S(1)} copy-done((f32[64,8,128]{2,1,0:T(8,128)S(1)}, f32[64,8,128]{2,1,0:T(8,128)}, u32[]{:S(2)}) %copy-start.4) | copy-done | bytes 262168
  8.9 0.0 copy-start.5
  8.9 0.9 %copy-done.5 = bf16[2,2,128,128]{3,2,1,0:T(8,128)(2,1)S(1)} copy-done((bf16[2,2,128,128]{3,2,1,0:T(8,128)(2,1)S(1)}, bf16[2,2,128,128]{3,2,1,0:T(8,128)(2,1)}, u32[]{:S(2)}) %copy-start.5) | copy-done | bytes 131096
  9.8 0.0 copy-start.6
  9.8 0.8 %copy-done.6 = bf16[128,128]{1,0:T(8,128)(2,1)S(1)} copy-done((bf16[128,128]{1,0:T(8,128)(2,1)S(1)}, bf16[128,128]{1,0:T(8,128)(2,1)}, u32[]{:S(2)}) %copy-start.6) | copy-done | bytes 32792
  10.5 0.0 copy-start.7
  10.5 0.7 copy-done.7
  11.2 0.0 copy-start.8
  11.2 0.7 copy-done.8
  11.9 0.7 copy-done.9
  12.5 0.7 copy-done.10
  13.2 55.3 %shard_map.139 = (f32[2,8,64,128]{3,2,1,0:T(8,128)S(1)}, f32[2,64,128]{2,1,0:T(8,128)S(1)}, f32[2,64,128]{2,1,0:T(8,128)S(1)}) custom-call(f32[8,64,32]{2,1,0:T(8,128)S(1)} %copy.15.trace_hbm, f32[8]{0:T(128)S(1)} %copy-done.8, f32[8]{0:T(128)S(1)} %copy-done.9, f32[8]{0:T(128)S(1)} %copy-done.10, f32[64,8,128]{2,1,0:T(8,128)S(1)} %copy-done.4, ...), custom_call_target="tpu_custom_call" | custom-call | tf_op jit(solution)/shard_map/pallas_call | solution.py:455
  68.5 0.8 %copy.20 = f32[2,8,64,128]{3,2,1,0:T(8,128)} copy(f32[2,8,64,128]{3,2,1,0:T(8,128)S(1)} %get-tuple-element.15) | data formatting | bytes 1048576
  69.3 0.6 copy.21
  69.9 0.6 copy.22
  (3 shorter events, 0.0 us)
Async XLA Ops:
  1.7 3.4 %copy-start = (bf16[64,2,2,128,128]{4,3,2,1,0:T(8,128)(2,1)S(1)}, bf16[64,2,2,128,128]{4,3,2,1,0:T(8,128)(2,1)}, u32[]{:S(2)}) copy-start(bf16[64,2,2,128,128]{4,3,2,1,0:T(8,128)(2,1)} %constant.17.clone.middle_hbm) | copy-start | bytes 25165828
  5.1 1.0 %copy-start.1 = (bf16[2,128,640]{2,1,0:T(8,128)(2,1)S(1)}, bf16[2,128,640]{2,1,0:T(8,128)(2,1)}, u32[]{:S(2)}) copy-start(bf16[2,128,640]{2,1,0:T(8,128)(2,1)} %constant.20.clone.spread_hbm) | copy-start | bytes 983044
  6.0 0.9 %copy-start.2 = (bf16[2,256,256]{2,1,0:T(8,128)(2,1)S(1)}, bf16[2,256,256]{2,1,0:T(8,128)(2,1)}, u32[]{:S(2)}) copy-start(bf16[2,256,256]{2,1,0:T(8,128)(2,1)} %constant.22.clone.last_hbm) | copy-start | bytes 786436
  7.0 0.9 %copy-start.3 = (f32[8,64,128]{2,1,0:T(8,128)S(1)}, f32[8,64,128]{2,1,0:T(8,128)}, u32[]{:S(2)}) copy-start(f32[8,64,128]{2,1,0:T(8,128)} %constant.19.clone.twists_hbm) | copy-start | bytes 786436
  7.9 0.9 %copy-start.4 = (f32[64,8,128]{2,1,0:T(8,128)S(1)}, f32[64,8,128]{2,1,0:T(8,128)}, u32[]{:S(2)}) copy-start(f32[64,8,128]{2,1,0:T(8,128)} %constant.16.clone.vectors_hbm) | copy-start | bytes 786436
  8.9 0.9 %copy-start.5 = (bf16[2,2,128,128]{3,2,1,0:T(8,128)(2,1)S(1)}, bf16[2,2,128,128]{3,2,1,0:T(8,128)(2,1)}, u32[]{:S(2)}) copy-start(bf16[2,2,128,128]{3,2,1,0:T(8,128)(2,1)} %constant.18.clone.first_hbm) | copy-start | bytes 393220
  9.8 0.8 %copy-start.6 = (bf16[128,128]{1,0:T(8,128)(2,1)S(1)}, bf16[128,128]{1,0:T(8,128)(2,1)}, u32[]{:S(2)}) copy-start(bf16[128,128]{1,0:T(8,128)(2,1)} %constant.21.clone.mean_hbm) | copy-start | bytes 98308
  10.5 0.7 copy-start.7
  11.2 0.7 copy-start.8
  11.9 0.7 copy-start.9
  12.5 0.7 copy-start.10

commit v2 on v1

--- a/solution.py
+++ b/solution.py
@@ -116,6 +116,16 @@
     return jnp.dot(left, right, preferred_element_type=F32)
 
 
+def left_dot_turned(table, value):
+    high, low = parts_of(value)
+    return lax.dot_general(
+        jnp.concatenate([table[0], table[0], table[1]], axis=1),
+        jnp.concatenate([high, low, high], axis=1),
+        (((1,), (1,)), ((), ())),
+        preferred_element_type=F32,
+    )
+
+
 def right_dot(value, table):
     high, low = parts_of(value)
     left = jnp.concatenate([high, low, high], axis=1)
@@ -123,18 +133,27 @@
     return jnp.dot(left, right, preferred_element_type=F32)
 
 
+def ring_step(k, me):
+    yi, xi, zi = k & 7, (k >> 3) & 3, k >> 5
+    half = (yi + 1) >> 1
+    dy = 4 + half * (1 - 2 * (yi & 1))
+    dx = (xi ^ (xi >> 1)) ^ 2
+    dz = 1 - zi
+    return ((me + 8 * dy) & 56) | ((me + 2 * dx) & 6) | ((me ^ dz) & 1)
+
+
 def turn(real, imag, cosine, sine):
     return real * cosine - imag * sine, real * sine + imag * cosine
 
 
 def kernel(
-    trace_hbm, step_ref, pair_ref, chal_ref,
+    trace_hbm, step_hbm, pair_hbm, chal_hbm,
     vectors_hbm, middle_hbm, first_hbm, twists_hbm, spread_hbm, mean_hbm, last_hbm, scales_hbm,
-    ext_hbm, val_hbm, quot_hbm,
+    ext, val, quot,
     trace, vectors, middle, first, twists, spread, mean, last, scales,
-    ext, val, quot,
-    send1, recv1, send2, recv2, send3, recv3, send4, recv4, send5, recv5,
-    load_sems, store_sems, send_sems, recv_sems,
+    step_ref, pair_ref, chal_ref,
+    send1, recv1, send2, recv2, send3, recv3, send4, recv4, send5, recv5, send6, recv6,
+    load_sems, send_sems, recv_sems,
 ):
     me = lax.axis_index("row")
     col = lax.axis_index("col")
@@ -143,15 +162,18 @@
 
     def greet_row(k, carry):
         pl.semaphore_signal(
-            barrier, inc=1, device_id={"row": lax.rem(me + k, SEG)}, device_id_type=MESH
+            barrier, inc=1, device_id={"row": ring_step(k, me)}, device_id_type=MESH
         )
         return carry
 
     def greet_col(k, carry):
         pl.semaphore_signal(
-            barrier, inc=1, device_id={"col": lax.rem(col + k, COLS)}, device_id_type=MESH
+            barrier, inc=1, device_id={"col": (col + k) & 7}, device_id_type=MESH
         )
         return carry
+
+    lax.fori_loop(0, SEG - 1, greet_row, 0)
+    lax.fori_loop(1, COLS, greet_col, 0)
 
     loads = [
         pltpu.make_async_copy(src, dst, load_sems.at[i])
@@ -166,30 +188,31 @@
                 (mean_hbm, mean),
                 (scales_hbm, scales),
                 (last_hbm, last),
+                (step_hbm, step_ref),
+                (pair_hbm, pair_ref),
+                (chal_hbm, chal_ref),
             ]
         )
     ]
     for load in loads:
         load.start()
-    lax.fori_loop(1, SEG, greet_row, 0)
-    lax.fori_loop(1, COLS, greet_col, 0)
 
     loads[0].wait()
     loads[1].wait()
     grid = jnp.concatenate(
         [
-            jnp.concatenate([trace[2 * j + c] for j in range(PAIRS)], axis=1)
+            jnp.concatenate([trace[2 * j + c] for j in range(PAIRS)], axis=0)
             for c in range(2)
         ],
-        axis=0,
-    )
-    head = left_dot(first[0], grid)
+        axis=1,
+    )
+    head = left_dot_turned(first[0], grid)
     send1[...] = head.reshape(SEG, 2, LANES)
     recv1[me] = send1[me]
     pl.semaphore_wait(barrier, SEG - 1 + COLS - 1)
 
     def post1(k, carry):
-        peer = lax.rem(me + k, SEG)
+        peer = ring_step(k, me)
         pltpu.make_async_remote_copy(
             src_ref=send1.at[peer], dst_ref=recv1.at[me],
             send_sem=send_sems.at[0], recv_sem=recv_sems.at[0],
@@ -197,7 +220,7 @@
         ).start()
         return carry
 
-    lax.fori_loop(1, SEG, post1, 0)
+    lax.fori_loop(0, SEG - 1, post1, 0)
 
     for load in loads[2:]:
         load.wait()
@@ -239,7 +262,7 @@
         recv2[j, me] = send2[j, me]
 
     def post2(k, carry):
-        peer = lax.rem(me + k, SEG)
+        peer = ring_step(k, me)
         pltpu.make_async_remote_copy(
             src_ref=send2.at[:, peer], dst_ref=recv2.at[:, me],
             send_sem=send_sems.at[1], recv_sem=recv_sems.at[1],
@@ -247,7 +270,7 @@
         ).start()
         return carry
 
-    lax.fori_loop(1, SEG, post2, 0)
+    lax.fori_loop(0, SEG - 1, post2, 0)
     quot_cos, quot_sin = table(3, 3)
     pltpu.make_async_copy(
         recv2.at[:, pl.ds(0, SEG - 1)], recv2.at[:, pl.ds(0, SEG - 1)], recv_sems.at[1]
@@ -296,8 +319,6 @@
         level_ahead += chal_c * mean_d - chal_d * mean_c
         level_own += (chal_c - step_c) * mean_c + (chal_d - step_d) * mean_d
         level_product += weight * (mean_c * mean_d)
-    ext_copy = pltpu.make_async_copy(ext, ext_hbm, store_sems.at[0])
-    ext_copy.start()
     rim_sum = rim_part[:SEG] * rim_weight[0] + rim_part[SEG:] * rim_weight[1]
     rim_sum = rim_sum + pltpu.roll(rim_sum, 4, 1)
     rim_sum = rim_sum + pltpu.roll(rim_sum, 8, 1)
@@ -321,12 +342,12 @@
     )
     mixed = left_dot(first[0], jnp.concatenate([value_real, value_imag], axis=0))
     for i in range(COLS):
-        send3[i, 0:16] = mixed[16 * i : 16 * (i + 1)]
-        send3[i, 16:24] = value_real[8 * i : 8 * (i + 1)]
-        send3[i, 24:32] = value_imag[8 * i : 8 * (i + 1)]
+        send3[i] = mixed[16 * i : 16 * (i + 1)]
+        send6[i, 0:8] = value_real[8 * i : 8 * (i + 1)]
+        send6[i, 8:16] = value_imag[8 * i : 8 * (i + 1)]
 
     def post3(k, carry):
-        peer = lax.rem(col + k, COLS)
+        peer = (col + k) & 7
         pltpu.make_async_remote_copy(
             src_ref=send3.at[peer], dst_ref=recv3.at[col],
             send_sem=send_sems.at[2], recv_sem=recv_sems.at[2],
@@ -335,21 +356,32 @@
         return carry
 
     lax.fori_loop(1, COLS, post3, 0)
+
+    def post6(k, carry):
+        peer = (col + k) & 7
+        pltpu.make_async_remote_copy(
+            src_ref=send6.at[peer], dst_ref=recv6.at[col],
+            send_sem=send_sems.at[5], recv_sem=recv_sems.at[5],
+            device_id={"col": peer}, device_id_type=MESH,
+        ).start()
+        return carry
+
+    lax.fori_loop(1, COLS, post6, 0)
     recv3[col] = send3[col]
+    recv6[col] = send6[col]
     pltpu.make_async_copy(
         recv3.at[pl.ds(0, COLS - 1)], recv3.at[pl.ds(0, COLS - 1)], recv_sems.at[2]
     ).wait()
     total = recv3[0]
     for i in range(1, COLS):
         total = total + recv3[i]
-    send4[...] = total[:16].reshape(8, 2, LANES)
-    send5[...] = total[16:]
-
-    here = lax.div(me, COLS) == col
+    send4[...] = total.reshape(8, 2, LANES)
+
+    here = (me >> 3) == col
 
     def post4(k, carry):
-        line = lax.rem(lax.div(k, COLS) + me, COLS)
-        across = lax.rem(k + col, COLS)
+        line = (k + me) & 7
+        across = ((k >> 3) + col) & 7
         target = col * COLS + line
         alone = (target == me) & (across == col)
 
@@ -369,11 +401,19 @@
 
     lax.fori_loop(0, SEG, post4, 0)
 
+    pltpu.make_async_copy(
+        recv6.at[pl.ds(0, COLS - 1)], recv6.at[pl.ds(0, COLS - 1)], recv_sems.at[5]
+    ).wait()
+    value = recv6[0]
+    for i in range(1, COLS):
+        value = value + recv6[i]
+    send5[...] = value
+
     def post5(k, carry):
         pltpu.make_async_remote_copy(
             src_ref=send5, dst_ref=recv5.at[col],
             send_sem=send_sems.at[4], recv_sem=recv_sems.at[4],
-            device_id={"col": lax.rem(col + k, COLS)}, device_id_type=MESH,
+            device_id={"col": (col + k) & 7}, device_id_type=MESH,
         ).start()
         return carry
 
@@ -385,19 +425,11 @@
     real, imag = turn(mixed[:SEG], mixed[SEG:], quot_cos, quot_sin)
     both = jnp.concatenate([real, imag], axis=1)
     both = jnp.concatenate([both, both], axis=0)
-    high, low = parts_of(both)
-    result = lax.dot_general(
-        jnp.concatenate([last[0], last[0], last[1]], axis=1),
-        jnp.concatenate([high, low, high], axis=1),
-        (((1,), (1,)), ((), ())),
-        preferred_element_type=F32,
-    )
+    result = left_dot_turned(last, both)
     for c in range(2):
         even = result[LANES * c : LANES * c + SEG]
         odd = result[LANES * c + SEG : LANES * (c + 1)]
         quot[c] = jnp.where(lane < SEG, even, odd)
-    quot_copy = pltpu.make_async_copy(quot, quot_hbm, store_sems.at[1])
-    quot_copy.start()
 
     pltpu.make_async_copy(
         recv5.at[pl.ds(0, COLS - 1)], recv5.at[pl.ds(0, COLS - 1)], recv_sems.at[4]
@@ -405,8 +437,6 @@
     for i in range(COLS):
         val[0, 8 * i : 8 * (i + 1)] = recv5[i, 0:8]
         val[1, 8 * i : 8 * (i + 1)] = recv5[i, 8:16]
-    val_copy = pltpu.make_async_copy(val, val_hbm, store_sems.at[2])
-    val_copy.start()
 
     pltpu.make_async_copy(
         send1.at[pl.ds(0, SEG - 1)], send1.at[pl.ds(0, SEG - 1)], send_sems.at[0]
@@ -428,21 +458,35 @@
     def _():
         pltpu.make_async_copy(recv4, recv4, send_sems.at[3]).wait()
 
-    pltpu.make_async_copy(
-        recv5.at[pl.ds(0, COLS - 1)], recv5.at[pl.ds(0, COLS - 1)], send_sems.at[4]
-    ).wait()
-    ext_copy.wait()
-    quot_copy.wait()
-    val_copy.wait()
+    for i in (4, 5):
+        pltpu.make_async_copy(
+            recv5.at[pl.ds(0, COLS - 1)], recv5.at[pl.ds(0, COLS - 1)], send_sems.at[i]
+        ).wait()
+
+
+def carry_out(ext, val, quot, ext_out, val_out, quot_out, sems):
+    moves = [
+        pltpu.make_async_copy(src, dst, sems.at[i])
+        for i, (src, dst) in enumerate([(ext, ext_out), (val, val_out), (quot, quot_out)])
+    ]
+    for move in moves:
+        move.start()
+    for move in moves:
+        move.wait()
 
 
 def shards(trace, step_coeff, pair_coeff, challenges):
+    trace = trace.transpose(0, 2, 1)
     tables = build_tables()
     names = ["vectors", "middle", "first", "twists", "spread", "mean", "last", "scales"]
     constants = [jnp.asarray(tables[name]) for name in names]
+    operands = [
+        pltpu.with_memory_space_constraint(x, pltpu.HBM)
+        for x in (trace, step_coeff, pair_coeff, challenges, *constants)
+    ]
     vmem = pltpu.VMEM
-    anywhere = pl.BlockSpec(memory_space=pl.ANY)
-    scalar = pl.BlockSpec(memory_space=pltpu.SMEM)
+    hbm = pl.BlockSpec(memory_space=pltpu.HBM)
+    inside = pl.BlockSpec(memory_space=pltpu.VMEM)
     outs = (
         jax.ShapeDtypeStruct((2, COLS, SEG, LANES), F32),
         jax.ShapeDtypeStruct((2, SEG, LANES), F32),
@@ -454,32 +498,40 @@
     ]
     extension, values, quotient = pl.pallas_call(
         kernel,
-        out_shape=outs,
-        in_specs=[anywhere, scalar, scalar, scalar] + [anywhere] * len(constants),
-        out_specs=(anywhere,) * 3,
+        out_shape=tuple(vmem(o.shape, F32) for o in outs),
+        in_specs=[hbm] * (4 + len(constants)),
+        out_specs=(inside,) * 3,
         scratch_shapes=[
             vmem(trace.shape, F32),
             *tables_scratch,
-            *[vmem(o.shape, F32) for o in outs],
+            *[pltpu.SMEM((COLS,), F32)] * 3,
             vmem((SEG, 2, LANES), F32),
             vmem((SEG, 2, LANES), F32),
             vmem((5, SEG, 2, LANES), F32),
             vmem((5, SEG, 2, LANES), F32),
-            vmem((COLS, 32, LANES), F32),
-            vmem((COLS, 32, LANES), F32),
+            vmem((COLS, 16, LANES), F32),
+            vmem((COLS, 16, LANES), F32),
             vmem((8, 2, LANES), F32),
             vmem((SEG, 2, LANES), F32),
             vmem((16, LANES), F32),
             vmem((COLS, 16, LANES), F32),
-            pltpu.SemaphoreType.DMA((9,)),
-            pltpu.SemaphoreType.DMA((3,)),
-            pltpu.SemaphoreType.DMA((5,)),
-            pltpu.SemaphoreType.DMA((5,)),
+            vmem((COLS, 16, LANES), F32),
+            vmem((COLS, 16, LANES), F32),
+            pltpu.SemaphoreType.DMA((12,)),
+            pltpu.SemaphoreType.DMA((6,)),
+            pltpu.SemaphoreType.DMA((6,)),
         ],
         compiler_params=pltpu.CompilerParams(
             collective_id=0, has_side_effects=True, vmem_limit_bytes=32 * 1024 * 1024
         ),
-    )(trace, step_coeff, pair_coeff, challenges, *constants)
+    )(*operands)
+    extension, values, quotient = pl.pallas_call(
+        carry_out,
+        out_shape=outs,
+        in_specs=[inside] * 3,
+        out_specs=(hbm,) * 3,
+        scratch_shapes=[pltpu.SemaphoreType.DMA((3,))],
+    )(*[pltpu.with_memory_space_constraint(x, vmem) for x in (extension, values, quotient)])
     return extension, values, quotient.reshape(2, 1, SEG * LANES)
 
 

time: 71 us -> 53.2 us (0.75)
  local copies, waits for them, and re-layouts: 14.6 us -> 0 us
  Pallas kernels: 55.3 us -> 52.5 us
    unnamed x26 -> x0, local copies, waits for them, and re-layouts: 14.6 us -> none
    pallas_call x1 -> x2, Pallas kernels: 55.3 us -> 52.5 us  [the longest x1 51.6 us: shards(): pl.pallas_call(kernel, out_shape=tuple((vmem(o.shape, F32) for o in outs)...]
where the time goes in v2:
time: 53.2 us; the launch traced here: 53.1 us
  Pallas kernels  52.5 us (99%)
  between operations  0.64 us (1%)
    pallas_call x1, Pallas kernels, shards(): pl.pallas_call(kernel, out_shape=tuple((vmem(o.shape, F32) for o in outs)...  51.6 us

profile of v2, /device:TPU:1, one launch (start us, length us, event | category | flops | bytes accessed | tf_op | source)
XLA Modules:
  0.0 53.1 jit_solution(3120686575624964894)
XLA Ops:
  0.6 51.6 %shard_map.139 = (f32[2,8,64,128]{3,2,1,0:T(8,128)S(1)}, f32[2,64,128]{2,1,0:T(8,128)S(1)}, f32[2,64,128]{2,1,0:T(8,128)S(1)}) custom-call(f32[8,32,64]{2,1,0:T(8,128)} %bitcast.2, f32[8]{0:T(128)} %step_hbm.1, f32[8]{0:T(128)} %pair_hbm.1, f32[8]{0:T(128)} %chal_hbm.1, f32[64,8,128]{2,1,0:T(8,128)} %constant.16.clone.vectors_hbm, ...), custom_call_target="tpu_custom_call" | custom-call | tf_op jit(solution)/shard_map/pallas_call | solution.py:499
  52.2 0.9 %shard_map.140 = (f32[2,8,64,128]{3,2,1,0:T(8,128)}, f32[2,64,128]{2,1,0:T(8,128)}, f32[2,64,128]{2,1,0:T(8,128)}) custom-call(f32[2,8,64,128]{3,2,1,0:T(8,128)S(1)} %get-tuple-element.9.ext, f32[2,64,128]{2,1,0:T(8,128)S(1)} %get-tuple-element.10.val, f32[2,64,128]{2,1,0:T(8,128)S(1)} %get-tuple-element.11.quot), custom_call_target="tpu_custom_call" | custom-call | tf_op jit(solution)/shard_map/pallas_call | solution.py:528

commit v3 on v2

--- a/solution.py
+++ b/solution.py
@@ -9,6 +9,7 @@
 from jax.sharding import PartitionSpec as P
 
 SEG = 64
+HALF = 32
 COLS = 8
 PAIRS = 4
 RUN = 32
@@ -43,17 +44,18 @@
     seg = np.arange(SEG)
     run = np.arange(RUN)
     first = real_form(tau * np.outer(seg, seg) / SEG, "oc", "ci")
-    middle = []
-    vectors = []
+    final = first.T.reshape(2 * SEG, SEG // 2, 2, 2).transpose(0, 2, 1, 3).reshape(2 * SEG, 2 * SEG)
     lane = np.arange(LANES)
     offset = lane // 4 + (2 * (lane % 4) + 1) / 8.0
     rim = RUN + (2 * (lane % 4) + 1) / 8.0
     rim_here = (lane >= LANES - 16).astype(np.float64)
     beta = np.tile(run, PAIRS)
+    slots = np.concatenate([seg[0::2], seg[1::2]])
+    matrices = []
+    vectors = []
     for u in range(SEG):
-        angle = tau * np.outer(SEG * seg + u, seg) / (SEG * SEG)
-        matrix = real_form(angle, "co", "ic")
-        middle.append(np.stack([halves(matrix), halves(matrix.T)]))
+        angle = tau * np.outer(SEG * seg + u, slots) / (SEG * SEG)
+        matrices.append(real_form(angle, "co", "ic"))
         vectors.append(
             np.concatenate(
                 [
@@ -64,6 +66,15 @@
                 ]
             )
         )
+    into, outof, turns = [], [], []
+    for g in range(HALF):
+        pair = (2 * g, 2 * g + 1)
+        into.append(np.stack([halves(matrices[u]) for u in pair]))
+        for zh in range(2):
+            rows = slice(SEG * zh, SEG * (zh + 1))
+            outof.append(np.stack([halves(matrices[u].T[rows]) for u in pair]))
+            turns.append(np.concatenate([vectors[u][:6] for u in pair] + [vectors[2 * g + zh][6:]]))
+    vectors = np.pad(np.stack(turns), ((0, 0), (0, 2), (0, 0)))
     twist_in = complex_rows(tau * beta * (64 * seg[:, None] - 2048) / TRACE_LEN)
     twist_out = complex_rows(-tau * offset * (64 * seg[:, None] - 2048) / TRACE_LEN) / TRACE_LEN
     twist_rim = (
@@ -92,9 +103,10 @@
         scales += [value.real, value.imag]
     scales += [np.zeros(LANES)] * 2
     return {
-        "vectors": np.stack(vectors).astype(np.float32),
-        "middle": np.stack(middle),
-        "first": np.stack([halves(first), halves(first.T)]),
+        "vectors": vectors.astype(np.float32),
+        "into": np.stack(into),
+        "outof": np.stack(outof),
+        "first": np.stack([halves(first), halves(final)]),
         "twists": twists.astype(np.float32),
         "spread": halves(spread),
         "mean": mean.reshape(LANES, LANES).astype(BF16),
@@ -148,15 +160,17 @@
 
 def kernel(
     trace_hbm, step_hbm, pair_hbm, chal_hbm,
-    vectors_hbm, middle_hbm, first_hbm, twists_hbm, spread_hbm, mean_hbm, last_hbm, scales_hbm,
+    vectors_hbm, into_hbm, outof_hbm, first_hbm, twists_hbm, spread_hbm, mean_hbm, last_hbm, scales_hbm,
     ext, val, quot,
-    trace, vectors, middle, first, twists, spread, mean, last, scales,
+    trace, vectors, into, outof, first, twists, spread, mean, last, scales,
     step_ref, pair_ref, chal_ref,
     send1, recv1, send2, recv2, send3, recv3, send4, recv4, send5, recv5, send6, recv6,
-    load_sems, send_sems, recv_sems,
+    load_sems, send_sems, recv_sems, ready,
 ):
     me = lax.axis_index("row")
     col = lax.axis_index("col")
+    group, far = me >> 1, me & 1
+    slot = HALF * far + group
 
     barrier = pltpu.get_barrier_semaphore()
 
@@ -172,7 +186,11 @@
         )
         return carry
 
-    lax.fori_loop(0, SEG - 1, greet_row, 0)
+    @pl.when(far == 0)
+    def _():
+        lax.fori_loop(0, HALF, greet_row, 0)
+
+    lax.fori_loop(HALF, SEG - 1, greet_row, 0)
     lax.fori_loop(1, COLS, greet_col, 0)
 
     loads = [
@@ -182,7 +200,8 @@
                 (trace_hbm, trace),
                 (first_hbm, first),
                 (vectors_hbm.at[me], vectors),
-                (middle_hbm.at[me], middle),
+                (into_hbm.at[group], into),
+                (outof_hbm.at[me], outof),
                 (twists_hbm, twists),
                 (spread_hbm, spread),
                 (mean_hbm, mean),
@@ -208,75 +227,101 @@
     )
     head = left_dot_turned(first[0], grid)
     send1[...] = head.reshape(SEG, 2, LANES)
-    recv1[me] = send1[me]
-    pl.semaphore_wait(barrier, SEG - 1 + COLS - 1)
-
-    def post1(k, carry):
+    for c in range(2):
+        recv1[c, slot] = send1[2 * group + c]
+    pl.semaphore_wait(barrier, HALF - 1 + COLS - 1 + HALF * far)
+
+    def post1(k, to):
         peer = ring_step(k, me)
         pltpu.make_async_remote_copy(
-            src_ref=send1.at[peer], dst_ref=recv1.at[me],
-            send_sem=send_sems.at[0], recv_sem=recv_sems.at[0],
+            src_ref=send1.at[pl.ds(2 * (peer >> 1), 2)], dst_ref=recv1.at[:, slot],
+            send_sem=send_sems.at[to], recv_sem=recv_sems.at[to],
             device_id={"row": peer}, device_id_type=MESH,
         ).start()
-        return carry
-
-    lax.fori_loop(0, SEG - 1, post1, 0)
+        return to
+
+    @pl.when(far == 1)
+    def _():
+        pl.semaphore_signal(ready, inc=1, device_id={"row": me ^ 1}, device_id_type=MESH)
+        lax.fori_loop(0, HALF, post1, 6)
+
+    lax.fori_loop(HALF, SEG - 1, post1, 0)
 
     for load in loads[2:]:
         load.wait()
-    head_high, head_low = parts_of(head[:8])
-    sums = jnp.dot(head_high, mean[...], preferred_element_type=F32) + jnp.dot(
-        head_low, mean[...], preferred_element_type=F32
-    )
-    parity = lax.broadcasted_iota(jnp.int32, (LANES, LANES), 0) % 2
-    sums = jnp.where(parity == 0, sums[0:1], sums[1:2])
-
     def table(index, row):
         base = twists[2 * index], twists[2 * index + 1]
         return turn(*base, vectors[2 * row : 2 * row + 1], vectors[2 * row + 1 : 2 * row + 2])
 
-    in_cos, in_sin = table(0, 0)
-    out_cos, out_sin = table(1, 1)
-    rim_cos, rim_sin = table(2, 2)
-
-    pltpu.make_async_copy(
-        recv1.at[pl.ds(0, SEG - 1)], recv1.at[pl.ds(0, SEG - 1)], recv_sems.at[0]
-    ).wait()
-
-    mixed = left_dot(middle[0], recv1[...].reshape(LANES, LANES))
-    real, imag = turn(mixed[:SEG], mixed[SEG:], in_cos, in_sin)
-    wide = right_dot(jnp.concatenate([real, imag], axis=0), spread)
-    pieces = []
-    for j in range(5):
-        cosine, sine = (out_cos, out_sin) if j < 4 else (rim_cos, rim_sin)
-        part = wide[:, LANES * j : LANES * (j + 1)]
-        real, imag = turn(part[:SEG], part[SEG:], cosine, sine)
-        pieces.append(jnp.concatenate([real, imag], axis=0))
-    back = left_dot(middle[1], jnp.concatenate(pieces, axis=1))
-    for j in range(5):
-        part = back[:, LANES * j : LANES * (j + 1)]
-        if j == 4:
-            part = part + sums
-        send2[j] = part.reshape(SEG, 2, LANES)
-    for j in range(5):
-        recv2[j, me] = send2[j, me]
+    turn_in = [table(0, 3 * c) for c in range(2)]
+    turn_out = [table(1, 3 * c + 1) for c in range(2)]
+    turn_rim = [table(2, 3 * c + 2) for c in range(2)]
+
+    own_half = recv1.at[:, pl.ds(0, HALF - 1)]
+    pltpu.make_async_copy(own_half, own_half, recv_sems.at[0]).wait()
+    gathered = recv1.at[:, pl.ds(0, HALF)]
+
+    @pl.when(far == 0)
+    def _():
+        pl.semaphore_wait(ready, 1)
+        pltpu.make_async_remote_copy(
+            src_ref=gathered, dst_ref=gathered,
+            send_sem=send_sems.at[6], recv_sem=recv_sems.at[6],
+            device_id={"row": me ^ 1}, device_id_type=MESH,
+        ).start()
+
+    pltpu.make_async_copy(gathered, gathered, recv_sems.at[6]).wait()
+
+    rows = []
+    for c in range(2):
+        mixed = left_dot(into[c], recv1[c].reshape(LANES, LANES))
+        if c == 0:
+            lowest = jnp.concatenate([mixed[0:8], mixed[SEG : SEG + 8]], axis=0)
+        rows += turn(mixed[:SEG], mixed[SEG:], *turn_in[c])
+    wide = right_dot(jnp.concatenate(rows, axis=0), spread)
+    high, low = parts_of(lowest)
+    sums = jnp.dot(high, mean[...], preferred_element_type=F32) + jnp.dot(
+        low, mean[...], preferred_element_type=F32
+    )
+    sums = sums * jnp.where(group == 0, 1.0, 0.0).astype(F32)
+    parity = lax.broadcasted_iota(jnp.int32, (SEG, LANES), 0) % 2
+    sums = jnp.where(parity == 0, sums[0:1], sums[8:9])
+    for c in range(2):
+        pieces = []
+        for j in range(5):
+            part = wide[LANES * c : LANES * (c + 1), LANES * j : LANES * (j + 1)]
+            real, imag = turn(part[:SEG], part[SEG:], *(turn_out[c] if j < 4 else turn_rim[c]))
+            pieces.append(jnp.concatenate([real, imag], axis=0))
+        back = left_dot(outof[c], jnp.concatenate(pieces, axis=1))
+        for j in range(5):
+            part = back[:, LANES * j : LANES * (j + 1)]
+            if j == 4 and c == 0:
+                part = part + sums
+            send2[2 * j + c] = part.reshape(HALF, 2, LANES)
+    for i in range(10):
+        recv2[i, group] = send2[i, group]
 
     def post2(k, carry):
         peer = ring_step(k, me)
         pltpu.make_async_remote_copy(
-            src_ref=send2.at[:, peer], dst_ref=recv2.at[:, me],
+            src_ref=send2.at[:, peer >> 1], dst_ref=recv2.at[:, group],
             send_sem=send_sems.at[1], recv_sem=recv_sems.at[1],
             device_id={"row": peer}, device_id_type=MESH,
         ).start()
         return carry
 
-    lax.fori_loop(0, SEG - 1, post2, 0)
-    quot_cos, quot_sin = table(3, 3)
-    pltpu.make_async_copy(
-        recv2.at[:, pl.ds(0, SEG - 1)], recv2.at[:, pl.ds(0, SEG - 1)], recv_sems.at[1]
-    ).wait()
-
-    arrived = jnp.concatenate([recv2[j].reshape(LANES, LANES) for j in range(5)], axis=1)
+    lax.fori_loop(HALF, SEG - 1, post2, 0)
+    quot_cos, quot_sin = table(3, 6)
+    others = recv2.at[:, pl.ds(0, HALF - 1)]
+    pltpu.make_async_copy(others, others, recv_sems.at[1]).wait()
+
+    arrived = jnp.concatenate(
+        [
+            jnp.concatenate([recv2[2 * j + c].reshape(SEG, LANES) for c in range(2)], axis=0)
+            for j in range(5)
+        ],
+        axis=1,
+    )
     field = left_dot(first[1], arrived)
 
     def scale(row):
@@ -388,14 +433,14 @@
         @pl.when(jnp.logical_not(alone))
         def _():
             pltpu.make_async_remote_copy(
-                src_ref=send4.at[line], dst_ref=recv4.at[me],
+                src_ref=send4.at[line], dst_ref=recv4.at[slot],
                 send_sem=send_sems.at[3], recv_sem=recv_sems.at[3],
                 device_id={"col": across, "row": target}, device_id_type=MESH,
             ).start()
 
         @pl.when(alone)
         def _():
-            pltpu.make_async_copy(send4.at[line], recv4.at[me], recv_sems.at[3]).start()
+            pltpu.make_async_copy(send4.at[line], recv4.at[slot], recv_sems.at[3]).start()
 
         return carry
 
@@ -421,7 +466,7 @@
     recv5[col] = send5[...]
 
     pltpu.make_async_copy(recv4, recv4, recv_sems.at[3]).wait()
-    mixed = left_dot(middle[0], recv4[...].reshape(LANES, LANES))
+    mixed = left_dot(into[far], recv4[...].reshape(LANES, LANES))
     real, imag = turn(mixed[:SEG], mixed[SEG:], quot_cos, quot_sin)
     both = jnp.concatenate([real, imag], axis=1)
     both = jnp.concatenate([both, both], axis=0)
@@ -438,12 +483,9 @@
         val[0, 8 * i : 8 * (i + 1)] = recv5[i, 0:8]
         val[1, 8 * i : 8 * (i + 1)] = recv5[i, 8:16]
 
-    pltpu.make_async_copy(
-        send1.at[pl.ds(0, SEG - 1)], send1.at[pl.ds(0, SEG - 1)], send_sems.at[0]
-    ).wait()
-    pltpu.make_async_copy(
-        send2.at[:, pl.ds(0, SEG - 1)], send2.at[:, pl.ds(0, SEG - 1)], send_sems.at[1]
-    ).wait()
+    pltpu.make_async_copy(own_half, own_half, send_sems.at[0]).wait()
+    pltpu.make_async_copy(gathered, gathered, send_sems.at[6]).wait()
+    pltpu.make_async_copy(others, others, send_sems.at[1]).wait()
     pltpu.make_async_copy(
         send3.at[pl.ds(0, COLS - 1)], send3.at[pl.ds(0, COLS - 1)], send_sems.at[2]
     ).wait()
@@ -478,7 +520,7 @@
 def shards(trace, step_coeff, pair_coeff, challenges):
     trace = trace.transpose(0, 2, 1)
     tables = build_tables()
-    names = ["vectors", "middle", "first", "twists", "spread", "mean", "last", "scales"]
+    names = ["vectors", "into", "outof", "first", "twists", "spread", "mean", "last", "scales"]
     constants = [jnp.asarray(tables[name]) for name in names]
     operands = [
         pltpu.with_memory_space_constraint(x, pltpu.HBM)
@@ -493,7 +535,7 @@
         jax.ShapeDtypeStruct((2, SEG, LANES), F32),
     )
     tables_scratch = [
-        vmem(c.shape[1:] if n in ("vectors", "middle") else c.shape, c.dtype)
+        vmem(c.shape[1:] if n in ("vectors", "into", "outof") else c.shape, c.dtype)
         for n, c in zip(names, constants, strict=True)
     ]
     extension, values, quotient = pl.pallas_call(
@@ -506,9 +548,9 @@
             *tables_scratch,
             *[pltpu.SMEM((COLS,), F32)] * 3,
             vmem((SEG, 2, LANES), F32),
-            vmem((SEG, 2, LANES), F32),
-            vmem((5, SEG, 2, LANES), F32),
-            vmem((5, SEG, 2, LANES), F32),
+            vmem((2, SEG, 2, LANES), F32),
+            vmem((10, HALF, 2, LANES), F32),
+            vmem((10, HALF, 2, LANES), F32),
             vmem((COLS, 16, LANES), F32),
             vmem((COLS, 16, LANES), F32),
             vmem((8, 2, LANES), F32),
@@ -517,9 +559,10 @@
             vmem((COLS, 16, LANES), F32),
             vmem((COLS, 16, LANES), F32),
             vmem((COLS, 16, LANES), F32),
-            pltpu.SemaphoreType.DMA((12,)),
-            pltpu.SemaphoreType.DMA((6,)),
-            pltpu.SemaphoreType.DMA((6,)),
+            pltpu.SemaphoreType.DMA((13,)),
+            pltpu.SemaphoreType.DMA((7,)),
+            pltpu.SemaphoreType.DMA((7,)),
+            pltpu.SemaphoreType.REGULAR,
         ],
         compiler_params=pltpu.CompilerParams(
             collective_id=0, has_side_effects=True, vmem_limit_bytes=32 * 1024 * 1024

time: 53.2 us -> 50.8 us (0.955)
  Pallas kernels: 52.5 us -> 50 us
    pallas_call x1, Pallas kernels: 51.6 us -> 49.2 us  [shards(): pl.pallas_call(kernel, out_shape=tuple((vmem(o.shape, F32) for o in outs)...]
where the time goes in v3:
time: 50.8 us; the launch traced here: 50.7 us
  Pallas kernels  50 us (98%)
  between operations  0.64 us (1%)
    pallas_call x1, Pallas kernels, shards(): pl.pallas_call(kernel, out_shape=tuple((vmem(o.shape, F32) for o in outs)...  49.2 us

profile of v3, /device:TPU:1, one launch (start us, length us, event | category | flops | bytes accessed | tf_op | source)
XLA Modules:
  0.0 50.7 jit_solution(43173812562228652)
XLA Ops:
  0.6 49.2 %shard_map.148 = (f32[2,8,64,128]{3,2,1,0:T(8,128)S(1)}, f32[2,64,128]{2,1,0:T(8,128)S(1)}, f32[2,64,128]{2,1,0:T(8,128)S(1)}) custom-call(f32[8,32,64]{2,1,0:T(8,128)} %bitcast.2, f32[8]{0:T(128)} %step_hbm.1, f32[8]{0:T(128)} %pair_hbm.1, f32[8]{0:T(128)} %chal_hbm.1, f32[64,16,128]{2,1,0:T(8,128)} %constant.18.clone.vectors_hbm, ...), custom_call_target="tpu_custom_call" | custom-call | tf_op jit(solution)/shard_map/pallas_call | solution.py:541
  49.8 0.9 %shard_map.149 = (f32[2,8,64,128]{3,2,1,0:T(8,128)}, f32[2,64,128]{2,1,0:T(8,128)}, f32[2,64,128]{2,1,0:T(8,128)}) custom-call(f32[2,8,64,128]{3,2,1,0:T(8,128)S(1)} %get-tuple-element.9.ext, f32[2,64,128]{2,1,0:T(8,128)S(1)} %get-tuple-element.10.val, f32[2,64,128]{2,1,0:T(8,128)S(1)} %get-tuple-element.11.quot), custom_call_target="tpu_custom_call" | custom-call | tf_op jit(solution)/shard_map/pallas_call | solution.py:571

commit v4 on v3

--- a/solution.py
+++ b/solution.py
@@ -50,6 +50,8 @@
     rim = RUN + (2 * (lane % 4) + 1) / 8.0
     rim_here = (lane >= LANES - 16).astype(np.float64)
     beta = np.tile(run, PAIRS)
+    deal = np.array([dealt(m, i) for i in range(COLS) for m in range(8)])
+    summed = first.reshape(SEG, 2, 2 * SEG)[deal].reshape(2 * SEG, 2 * SEG)
     slots = np.concatenate([seg[0::2], seg[1::2]])
     matrices = []
     vectors = []
@@ -106,7 +108,7 @@
         "vectors": vectors.astype(np.float32),
         "into": np.stack(into),
         "outof": np.stack(outof),
-        "first": np.stack([halves(first), halves(final)]),
+        "first": np.stack([halves(first), halves(final), halves(summed)]),
         "twists": twists.astype(np.float32),
         "spread": halves(spread),
         "mean": mean.reshape(LANES, LANES).astype(BF16),
@@ -152,6 +154,10 @@
     dx = (xi ^ (xi >> 1)) ^ 2
     dz = 1 - zi
     return ((me + 8 * dy) & 56) | ((me + 2 * dx) & 6) | ((me ^ dz) & 1)
+
+
+def dealt(m, col):
+    return 8 * m + 2 * ((m + (col >> 1)) & 3) + (((m >> 2) ^ col) & 1)
 
 
 def turn(real, imag, cosine, sine):
@@ -186,12 +192,13 @@
         )
         return carry
 
+    lax.fori_loop(HALF, SEG - 1, greet_row, 0)
+    lax.fori_loop(1, COLS, greet_col, 0)
+
     @pl.when(far == 0)
     def _():
         lax.fori_loop(0, HALF, greet_row, 0)
 
-    lax.fori_loop(HALF, SEG - 1, greet_row, 0)
-    lax.fori_loop(1, COLS, greet_col, 0)
 
     loads = [
         pltpu.make_async_copy(src, dst, load_sems.at[i])
@@ -295,10 +302,13 @@
         back = left_dot(outof[c], jnp.concatenate(pieces, axis=1))
         for j in range(5):
             part = back[:, LANES * j : LANES * (j + 1)]
-            if j == 4 and c == 0:
-                part = part + sums
-            send2[2 * j + c] = part.reshape(HALF, 2, LANES)
-    for i in range(10):
+            if j < 4:
+                send2[2 * j + c] = part.reshape(HALF, 2, LANES)
+            elif c == 0:
+                rest = part + sums
+            else:
+                send2[8] = (rest + pltpu.roll(part, SEG, 1)).reshape(HALF, 2, LANES)
+    for i in range(9):
         recv2[i, group] = send2[i, group]
 
     def post2(k, carry):
@@ -315,12 +325,10 @@
     others = recv2.at[:, pl.ds(0, HALF - 1)]
     pltpu.make_async_copy(others, others, recv_sems.at[1]).wait()
 
+    blocks = [recv2[i].reshape(SEG, LANES) for i in range(9)]
+    blocks.append(pltpu.roll(blocks[8], SEG, 1))
     arrived = jnp.concatenate(
-        [
-            jnp.concatenate([recv2[2 * j + c].reshape(SEG, LANES) for c in range(2)], axis=0)
-            for j in range(5)
-        ],
-        axis=1,
+        [jnp.concatenate(blocks[2 * j : 2 * j + 2], axis=0) for j in range(5)], axis=1
     )
     field = left_dot(first[1], arrived)
 
@@ -385,7 +393,7 @@
         - square_scale[0] * square_imag
         - square_scale[1] * square_real
     )
-    mixed = left_dot(first[0], jnp.concatenate([value_real, value_imag], axis=0))
+    mixed = left_dot(first[2], jnp.concatenate([value_real, value_imag], axis=0))
     for i in range(COLS):
         send3[i] = mixed[16 * i : 16 * (i + 1)]
         send6[i, 0:8] = value_real[8 * i : 8 * (i + 1)]
@@ -422,12 +430,12 @@
         total = total + recv3[i]
     send4[...] = total.reshape(8, 2, LANES)
 
-    here = (me >> 3) == col
+    here = dealt(me >> 3, col) == me
 
     def post4(k, carry):
-        line = (k + me) & 7
-        across = ((k >> 3) + col) & 7
-        target = col * COLS + line
+        line = (((k & 3) + (me >> 3)) & 3) | ((((k >> 5) ^ col) & 1) << 2)
+        across = ((k >> 2) + col) & 7
+        target = dealt(line, col)
         alone = (target == me) & (across == col)
 
         @pl.when(jnp.logical_not(alone))
@@ -507,10 +515,9 @@
 
 
 def carry_out(ext, val, quot, ext_out, val_out, quot_out, sems):
-    moves = [
-        pltpu.make_async_copy(src, dst, sems.at[i])
-        for i, (src, dst) in enumerate([(ext, ext_out), (val, val_out), (quot, quot_out)])
-    ]
+    pieces = [(ext.at[:, c], ext_out.at[:, c]) for c in range(COLS)]
+    pieces += [(val, val_out), (quot, quot_out)]
+    moves = [pltpu.make_async_copy(src, dst, sems.at[i]) for i, (src, dst) in enumerate(pieces)]
     for move in moves:
         move.start()
     for move in moves:
@@ -549,8 +556,8 @@
             *[pltpu.SMEM((COLS,), F32)] * 3,
             vmem((SEG, 2, LANES), F32),
             vmem((2, SEG, 2, LANES), F32),
-            vmem((10, HALF, 2, LANES), F32),
-            vmem((10, HALF, 2, LANES), F32),
+            vmem((9, HALF, 2, LANES), F32),
+            vmem((9, HALF, 2, LANES), F32),
             vmem((COLS, 16, LANES), F32),
             vmem((COLS, 16, LANES), F32),
             vmem((8, 2, LANES), F32),
@@ -573,7 +580,7 @@
         out_shape=outs,
         in_specs=[inside] * 3,
         out_specs=(hbm,) * 3,
-        scratch_shapes=[pltpu.SemaphoreType.DMA((3,))],
+        scratch_shapes=[pltpu.SemaphoreType.DMA((COLS + 2,))],
     )(*[pltpu.with_memory_space_constraint(x, vmem) for x in (extension, values, quotient)])
     return extension, values, quotient.reshape(2, 1, SEG * LANES)
 

time: 50.8 us -> 49.2 us (0.969)
  Pallas kernels: 50 us -> 48.4 us
    pallas_call x1, Pallas kernels: 49.2 us -> 47.5 us  [shards(): pl.pallas_call(kernel, out_shape=tuple((vmem(o.shape, F32) for o in outs)...]
where the time goes in v4:
time: 49.2 us; the launch traced here: 49 us
  Pallas kernels  48.4 us (98%)
  between operations  0.64 us (1%)
    pallas_call x1, Pallas kernels, shards(): pl.pallas_call(kernel, out_shape=tuple((vmem(o.shape, F32) for o in outs)...  47.5 us

profile of v4, /device:TPU:1, one launch (start us, length us, event | category | flops | bytes accessed | tf_op | source)
XLA Modules:
  0.0 49.0 jit_solution(1048947241771628025)
XLA Ops:
  0.6 47.5 %shard_map.148 = (f32[2,8,64,128]{3,2,1,0:T(8,128)S(1)}, f32[2,64,128]{2,1,0:T(8,128)S(1)}, f32[2,64,128]{2,1,0:T(8,128)S(1)}) custom-call(f32[8,32,64]{2,1,0:T(8,128)} %bitcast.2, f32[8]{0:T(128)} %step_hbm.1, f32[8]{0:T(128)} %pair_hbm.1, f32[8]{0:T(128)} %chal_hbm.1, f32[64,16,128]{2,1,0:T(8,128)} %constant.18.clone.vectors_hbm, ...), custom_call_target="tpu_custom_call" | custom-call | tf_op jit(solution)/shard_map/pallas_call | solution.py:548
  48.1 0.9 %shard_map.149 = (f32[2,8,64,128]{3,2,1,0:T(8,128)}, f32[2,64,128]{2,1,0:T(8,128)}, f32[2,64,128]{2,1,0:T(8,128)}) custom-call(f32[2,8,64,128]{3,2,1,0:T(8,128)S(1)} %get-tuple-element.9.ext, f32[2,64,128]{2,1,0:T(8,128)S(1)} %get-tuple-element.10.val, f32[2,64,128]{2,1,0:T(8,128)S(1)} %get-tuple-element.11.quot), custom_call_target="tpu_custom_call" | custom-call | tf_op jit(solution)/shard_map/pallas_call | solution.py:578

commit v5 on v4

--- a/solution.py
+++ b/solution.py
@@ -157,7 +157,7 @@
 
 
 def dealt(m, col):
-    return 8 * m + 2 * ((m + (col >> 1)) & 3) + (((m >> 2) ^ col) & 1)
+    return 8 * m + 2 * ((m + (col >> 1) + 2) & 3) + (((m >> 2) ^ col) & 1)
 
 
 def turn(real, imag, cosine, sine):
@@ -233,7 +233,7 @@
         axis=1,
     )
     head = left_dot_turned(first[0], grid)
-    send1[...] = head.reshape(SEG, 2, LANES)
+    send1.reshape(LANES, LANES)[...] = head
     for c in range(2):
         recv1[c, slot] = send1[2 * group + c]
     pl.semaphore_wait(barrier, HALF - 1 + COLS - 1 + HALF * far)
@@ -281,7 +281,7 @@
 
     rows = []
     for c in range(2):
-        mixed = left_dot(into[c], recv1[c].reshape(LANES, LANES))
+        mixed = left_dot(into[c], recv1.reshape(2, LANES, LANES)[c])
         if c == 0:
             lowest = jnp.concatenate([mixed[0:8], mixed[SEG : SEG + 8]], axis=0)
         rows += turn(mixed[:SEG], mixed[SEG:], *turn_in[c])
@@ -303,11 +303,11 @@
         for j in range(5):
             part = back[:, LANES * j : LANES * (j + 1)]
             if j < 4:
-                send2[2 * j + c] = part.reshape(HALF, 2, LANES)
+                send2.reshape(9, SEG, LANES)[2 * j + c] = part
             elif c == 0:
                 rest = part + sums
             else:
-                send2[8] = (rest + pltpu.roll(part, SEG, 1)).reshape(HALF, 2, LANES)
+                send2.reshape(9, SEG, LANES)[8] = rest + pltpu.roll(part, SEG, 1)
     for i in range(9):
         recv2[i, group] = send2[i, group]
 
@@ -325,7 +325,7 @@
     others = recv2.at[:, pl.ds(0, HALF - 1)]
     pltpu.make_async_copy(others, others, recv_sems.at[1]).wait()
 
-    blocks = [recv2[i].reshape(SEG, LANES) for i in range(9)]
+    blocks = [recv2.reshape(9, SEG, LANES)[i] for i in range(9)]
     blocks.append(pltpu.roll(blocks[8], SEG, 1))
     arrived = jnp.concatenate(
         [jnp.concatenate(blocks[2 * j : 2 * j + 2], axis=0) for j in range(5)], axis=1
@@ -343,6 +343,7 @@
     product = jnp.zeros((SEG, LANES), F32)
     cross = jnp.zeros((SEG, LANES), F32)
     rim_weight = [jnp.zeros((SEG, LANES), F32)] * 2
+    columns = []
     level_ahead = jnp.zeros((1, 1), F32)
     level_own = jnp.zeros((1, 1), F32)
     level_product = jnp.zeros((1, 1), F32)
@@ -356,10 +357,7 @@
         raw_d = field[SEG:, LANES * j : LANES * (j + 1)]
         real_c = raw_c + mean_d
         real_d = raw_d - mean_c
-        ext[0, 2 * j] = gain_real * real_c - gain_imag * mean_c
-        ext[1, 2 * j] = gain_imag * real_c + gain_real * mean_c
-        ext[0, 2 * j + 1] = gain_real * real_d - gain_imag * mean_d
-        ext[1, 2 * j + 1] = gain_imag * real_d + gain_real * mean_d
+        columns += [(real_c, mean_c), (real_d, mean_d)]
         ahead += chal_c * raw_c + chal_d * raw_d
         own += step_c * real_c + step_d * real_d
         product += weight * (real_c * real_d)
@@ -396,8 +394,6 @@
     mixed = left_dot(first[2], jnp.concatenate([value_real, value_imag], axis=0))
     for i in range(COLS):
         send3[i] = mixed[16 * i : 16 * (i + 1)]
-        send6[i, 0:8] = value_real[8 * i : 8 * (i + 1)]
-        send6[i, 8:16] = value_imag[8 * i : 8 * (i + 1)]
 
     def post3(k, carry):
         peer = (col + k) & 7
@@ -409,6 +405,9 @@
         return carry
 
     lax.fori_loop(1, COLS, post3, 0)
+    for i in range(COLS):
+        send6[i, 0:8] = value_real[8 * i : 8 * (i + 1)]
+        send6[i, 8:16] = value_imag[8 * i : 8 * (i + 1)]
 
     def post6(k, carry):
         peer = (col + k) & 7
@@ -422,19 +421,22 @@
     lax.fori_loop(1, COLS, post6, 0)
     recv3[col] = send3[col]
     recv6[col] = send6[col]
+    for c, (real, mean_here) in enumerate(columns):
+        ext[0, c] = gain_real * real - gain_imag * mean_here
+        ext[1, c] = gain_imag * real + gain_real * mean_here
     pltpu.make_async_copy(
         recv3.at[pl.ds(0, COLS - 1)], recv3.at[pl.ds(0, COLS - 1)], recv_sems.at[2]
     ).wait()
     total = recv3[0]
     for i in range(1, COLS):
         total = total + recv3[i]
-    send4[...] = total.reshape(8, 2, LANES)
+    send4.reshape(16, LANES)[...] = total
 
     here = dealt(me >> 3, col) == me
 
     def post4(k, carry):
-        line = (((k & 3) + (me >> 3)) & 3) | ((((k >> 5) ^ col) & 1) << 2)
-        across = ((k >> 2) + col) & 7
+        across = ((k >> 2) & 7) ^ 1
+        line = (k & 3) ^ (7 * (((k >> 5) ^ col) & 1))
         target = dealt(line, col)
         alone = (target == me) & (across == col)
 
@@ -453,7 +455,6 @@
         return carry
 
     lax.fori_loop(0, SEG, post4, 0)
-
     pltpu.make_async_copy(
         recv6.at[pl.ds(0, COLS - 1)], recv6.at[pl.ds(0, COLS - 1)], recv_sems.at[5]
     ).wait()
@@ -474,7 +475,7 @@
     recv5[col] = send5[...]
 
     pltpu.make_async_copy(recv4, recv4, recv_sems.at[3]).wait()
-    mixed = left_dot(into[far], recv4[...].reshape(LANES, LANES))
+    mixed = left_dot(into[far], recv4.reshape(LANES, LANES)[...])
     real, imag = turn(mixed[:SEG], mixed[SEG:], quot_cos, quot_sin)
     both = jnp.concatenate([real, imag], axis=1)
     both = jnp.concatenate([both, both], axis=0)

time: 49.2 us -> 47.4 us (0.963)
  Pallas kernels: 48.4 us -> 46.6 us
    pallas_call x1, Pallas kernels: 47.5 us -> 45.7 us  [shards(): pl.pallas_call(kernel, out_shape=tuple((vmem(o.shape, F32) for o in outs)...]
where the time goes in v5:
time: 47.4 us; the launch traced here: 47.3 us
  Pallas kernels  46.6 us (98%)
  between operations  0.64 us (1%)
    pallas_call x1, Pallas kernels, shards(): pl.pallas_call(kernel, out_shape=tuple((vmem(o.shape, F32) for o in outs)...  45.7 us

profile of v5, /device:TPU:1, one launch (start us, length us, event | category | flops | bytes accessed | tf_op | source)
XLA Modules:
  0.0 47.3 jit_solution(4112023352571164626)
XLA Ops:
  0.6 45.7 %shard_map.148 = (f32[2,8,64,128]{3,2,1,0:T(8,128)S(1)}, f32[2,64,128]{2,1,0:T(8,128)S(1)}, f32[2,64,128]{2,1,0:T(8,128)S(1)}) custom-call(f32[8,32,64]{2,1,0:T(8,128)} %bitcast.2, f32[8]{0:T(128)} %step_hbm.1, f32[8]{0:T(128)} %pair_hbm.1, f32[8]{0:T(128)} %chal_hbm.1, f32[64,16,128]{2,1,0:T(8,128)} %constant.18.clone.vectors_hbm, ...), custom_call_target="tpu_custom_call" | custom-call | tf_op jit(solution)/shard_map/pallas_call | solution.py:549
  46.3 0.9 %shard_map.149 = (f32[2,8,64,128]{3,2,1,0:T(8,128)}, f32[2,64,128]{2,1,0:T(8,128)}, f32[2,64,128]{2,1,0:T(8,128)}) custom-call(f32[2,8,64,128]{3,2,1,0:T(8,128)S(1)} %get-tuple-element.9.ext, f32[2,64,128]{2,1,0:T(8,128)S(1)} %get-tuple-element.10.val, f32[2,64,128]{2,1,0:T(8,128)S(1)} %get-tuple-element.11.quot), custom_call_target="tpu_custom_call" | custom-call | tf_op jit(solution)/shard_map/pallas_call | solution.py:579

commit v6 on v5

--- a/solution.py
+++ b/solution.py
@@ -157,7 +157,7 @@
 
 
 def dealt(m, col):
-    return 8 * m + 2 * ((m + (col >> 1) + 2) & 3) + (((m >> 2) ^ col) & 1)
+    return 8 * m + 2 * ((m + (col >> 1) + 2) & 3) + (((m >> 2) ^ col ^ 1) & 1)
 
 
 def turn(real, imag, cosine, sine):
@@ -436,7 +436,7 @@
 
     def post4(k, carry):
         across = ((k >> 2) & 7) ^ 1
-        line = (k & 3) ^ (7 * (((k >> 5) ^ col) & 1))
+        line = (k & 3) ^ (7 * (((k >> 5) ^ col ^ 1) & 1))
         target = dealt(line, col)
         alone = (target == me) & (across == col)
 
@@ -516,8 +516,7 @@
 
 
 def carry_out(ext, val, quot, ext_out, val_out, quot_out, sems):
-    pieces = [(ext.at[:, c], ext_out.at[:, c]) for c in range(COLS)]
-    pieces += [(val, val_out), (quot, quot_out)]
+    pieces = [(ext, ext_out), (val, val_out), (quot, quot_out)]
     moves = [pltpu.make_async_copy(src, dst, sems.at[i]) for i, (src, dst) in enumerate(pieces)]
     for move in moves:
         move.start()
@@ -581,7 +580,7 @@
         out_shape=outs,
         in_specs=[inside] * 3,
         out_specs=(hbm,) * 3,
-        scratch_shapes=[pltpu.SemaphoreType.DMA((COLS + 2,))],
+        scratch_shapes=[pltpu.SemaphoreType.DMA((3,))],
     )(*[pltpu.with_memory_space_constraint(x, vmem) for x in (extension, values, quotient)])
     return extension, values, quotient.reshape(2, 1, SEG * LANES)
 

time: 47.4 us -> 46.8 us (0.987)
  Pallas kernels: 46.6 us -> 46.1 us
    pallas_call x1, Pallas kernels: 45.7 us -> 45.2 us  [shards(): pl.pallas_call(kernel, out_shape=tuple((vmem(o.shape, F32) for o in outs)...]
where the time goes in v6:
time: 46.8 us; the launch traced here: 46.7 us
  Pallas kernels  46.1 us (99%)
  between operations  0.64 us (1%)
    pallas_call x1, Pallas kernels, shards(): pl.pallas_call(kernel, out_shape=tuple((vmem(o.shape, F32) for o in outs)...  45.2 us

profile of v6, /device:TPU:1, one launch (start us, length us, event | category | flops | bytes accessed | tf_op | source)
XLA Modules:
  0.0 46.7 jit_solution(14115537771390339710)
XLA Ops:
  0.6 45.2 %shard_map.148 = (f32[2,8,64,128]{3,2,1,0:T(8,128)S(1)}, f32[2,64,128]{2,1,0:T(8,128)S(1)}, f32[2,64,128]{2,1,0:T(8,128)S(1)}) custom-call(f32[8,32,64]{2,1,0:T(8,128)} %bitcast.2, f32[8]{0:T(128)} %step_hbm.1, f32[8]{0:T(128)} %pair_hbm.1, f32[8]{0:T(128)} %chal_hbm.1, f32[64,16,128]{2,1,0:T(8,128)} %constant.18.clone.vectors_hbm, ...), custom_call_target="tpu_custom_call" | custom-call | tf_op jit(solution)/shard_map/pallas_call | solution.py:548
  45.9 0.9 %shard_map.149 = (f32[2,8,64,128]{3,2,1,0:T(8,128)}, f32[2,64,128]{2,1,0:T(8,128)}, f32[2,64,128]{2,1,0:T(8,128)}) custom-call(f32[2,8,64,128]{3,2,1,0:T(8,128)S(1)} %get-tuple-element.9.ext, f32[2,64,128]{2,1,0:T(8,128)S(1)} %get-tuple-element.10.val, f32[2,64,128]{2,1,0:T(8,128)S(1)} %get-tuple-element.11.quot), custom_call_target="tpu_custom_call" | custom-call | tf_op jit(solution)/shard_map/pallas_call | solution.py:578

commit v7 on v6

--- a/solution.py
+++ b/solution.py
@@ -167,8 +167,8 @@
 def kernel(
     trace_hbm, step_hbm, pair_hbm, chal_hbm,
     vectors_hbm, into_hbm, outof_hbm, first_hbm, twists_hbm, spread_hbm, mean_hbm, last_hbm, scales_hbm,
-    ext, val, quot,
-    trace, vectors, into, outof, first, twists, spread, mean, last, scales,
+    ext, val, arrived_rows, own_into, last, spin,
+    trace, vectors, into, outof, first, twists, spread, mean, scales,
     step_ref, pair_ref, chal_ref,
     send1, recv1, send2, recv2, send3, recv3, send4, recv4, send5, recv5, send6, recv6,
     load_sems, send_sems, recv_sems, ready,
@@ -321,7 +321,8 @@
         return carry
 
     lax.fori_loop(HALF, SEG - 1, post2, 0)
-    quot_cos, quot_sin = table(3, 6)
+    spin[0], spin[1] = table(3, 6)
+    own_into[...] = into[far]
     others = recv2.at[:, pl.ds(0, HALF - 1)]
     pltpu.make_async_copy(others, others, recv_sems.at[1]).wait()
 
@@ -475,16 +476,7 @@
     recv5[col] = send5[...]
 
     pltpu.make_async_copy(recv4, recv4, recv_sems.at[3]).wait()
-    mixed = left_dot(into[far], recv4.reshape(LANES, LANES)[...])
-    real, imag = turn(mixed[:SEG], mixed[SEG:], quot_cos, quot_sin)
-    both = jnp.concatenate([real, imag], axis=1)
-    both = jnp.concatenate([both, both], axis=0)
-    result = left_dot_turned(last, both)
-    for c in range(2):
-        even = result[LANES * c : LANES * c + SEG]
-        odd = result[LANES * c + SEG : LANES * (c + 1)]
-        quot[c] = jnp.where(lane < SEG, even, odd)
-
+    arrived_rows[...] = recv4.reshape(LANES, LANES)[...]
     pltpu.make_async_copy(
         recv5.at[pl.ds(0, COLS - 1)], recv5.at[pl.ds(0, COLS - 1)], recv_sems.at[4]
     ).wait()
@@ -515,11 +507,24 @@
         ).wait()
 
 
-def carry_out(ext, val, quot, ext_out, val_out, quot_out, sems):
-    pieces = [(ext, ext_out), (val, val_out), (quot, quot_out)]
-    moves = [pltpu.make_async_copy(src, dst, sems.at[i]) for i, (src, dst) in enumerate(pieces)]
-    for move in moves:
-        move.start()
+def finish(
+    ext, val, arrived_rows, own_into, last, spin, ext_out, val_out, quot_out, quot, sems
+):
+    pairs = [(ext, ext_out), (val, val_out), (quot, quot_out)]
+    moves = [pltpu.make_async_copy(src, dst, sems.at[i]) for i, (src, dst) in enumerate(pairs)]
+    moves[0].start()
+    moves[1].start()
+    mixed = left_dot(own_into, arrived_rows[...])
+    real, imag = turn(mixed[:SEG], mixed[SEG:], spin[0], spin[1])
+    both = jnp.concatenate([real, imag], axis=1)
+    both = jnp.concatenate([both, both], axis=0)
+    result = left_dot_turned(last, both)
+    lane = lax.broadcasted_iota(jnp.int32, (SEG, LANES), 1)
+    for c in range(2):
+        even = result[LANES * c : LANES * c + SEG]
+        odd = result[LANES * c + SEG : LANES * (c + 1)]
+        quot[c] = jnp.where(lane < SEG, even, odd)
+    moves[2].start()
     for move in moves:
         move.wait()
 
@@ -544,12 +549,20 @@
     tables_scratch = [
         vmem(c.shape[1:] if n in ("vectors", "into", "outof") else c.shape, c.dtype)
         for n, c in zip(names, constants, strict=True)
+        if n != "last"
     ]
-    extension, values, quotient = pl.pallas_call(
+    passed = pl.pallas_call(
         kernel,
-        out_shape=tuple(vmem(o.shape, F32) for o in outs),
+        out_shape=(
+            vmem(outs[0].shape, F32),
+            vmem(outs[1].shape, F32),
+            vmem((LANES, LANES), F32),
+            vmem((2, LANES, LANES), BF16),
+            vmem((2, 2 * LANES, 2 * LANES), BF16),
+            vmem((2, SEG, LANES), F32),
+        ),
         in_specs=[hbm] * (4 + len(constants)),
-        out_specs=(inside,) * 3,
+        out_specs=(inside,) * 6,
         scratch_shapes=[
             vmem(trace.shape, F32),
             *tables_scratch,
@@ -576,12 +589,12 @@
         ),
     )(*operands)
     extension, values, quotient = pl.pallas_call(
-        carry_out,
+        finish,
         out_shape=outs,
-        in_specs=[inside] * 3,
+        in_specs=[inside] * 6,
         out_specs=(hbm,) * 3,
-        scratch_shapes=[pltpu.SemaphoreType.DMA((3,))],
-    )(*[pltpu.with_memory_space_constraint(x, vmem) for x in (extension, values, quotient)])
+        scratch_shapes=[vmem(outs[2].shape, F32), pltpu.SemaphoreType.DMA((3,))],
+    )(*[pltpu.with_memory_space_constraint(x, vmem) for x in passed])
     return extension, values, quotient.reshape(2, 1, SEG * LANES)
 
 

time: 46.8 us -> 46.6 us (level)
  no operation moved by 1% of the time
where the time goes in v7:
time: 46.6 us; the launch traced here: 46.4 us
  Pallas kernels  45.8 us (98%)
  between operations  0.64 us (1%)
    pallas_call x1, Pallas kernels, shards(): pl.pallas_call(kernel, out_shape=(vmem(outs[0].shape, F32), vmem(outs[1]....  44.7 us
    pallas_call x1, Pallas kernels, shards(): pl.pallas_call(finish, out_shape=outs, in_specs=[inside] * 6, out_specs=(...  1.09 us

profile of v7, /device:TPU:1, one launch (start us, length us, event | category | flops | bytes accessed | tf_op | source)
XLA Modules:
  0.0 46.4 jit_solution(13715789942161011716)
XLA Ops:
  0.6 44.7 %shard_map.148 = (f32[2,8,64,128]{3,2,1,0:T(8,128)S(1)}, f32[2,64,128]{2,1,0:T(8,128)S(1)}, f32[128,128]{1,0:T(8,128)S(1)}, bf16[2,128,128]{2,1,0:T(8,128)(2,1)S...) custom-call(f32[8,32,64]{2,1,0:T(8,128)} %bitcast.2, f32[8]{0:T(128)} %step_hbm.1, f32[8]{0:T(128)} %pair_hbm.1, ...), custom_call_target="tpu_custom_call" | custom-call | tf_op jit(solution)/shard_map/pallas_call | solution.py:554
  45.3 1.1 %shard_map.149 = (f32[2,8,64,128]{3,2,1,0:T(8,128)}, f32[2,64,128]{2,1,0:T(8,128)}, f32[2,64,128]{2,1,0:T(8,128)}) custom-call(f32[2,8,64,128]{3,2,1,0:T(8,128)S(1)} %get-tuple-element.12.ext, f32[2,64,128]{2,1,0:T(8,128)S(1)} %get-tuple-element.13.val, f32[128,128]{1,0:T(8,128)S(1)} %get-tuple-element.14.arrived_rows, ...), custom_call_target="tpu_custom_call" | custom-call | tf_op jit(solution)/shard_map/pallas_call | solution.py:591

commit v8 on v7

--- a/solution.py
+++ b/solution.py
@@ -308,9 +308,6 @@
                 rest = part + sums
             else:
                 send2.reshape(9, SEG, LANES)[8] = rest + pltpu.roll(part, SEG, 1)
-    for i in range(9):
-        recv2[i, group] = send2[i, group]
-
     def post2(k, carry):
         peer = ring_step(k, me)
         pltpu.make_async_remote_copy(
@@ -321,6 +318,8 @@
         return carry
 
     lax.fori_loop(HALF, SEG - 1, post2, 0)
+    for i in range(9):
+        recv2[i, group] = send2[i, group]
     spin[0], spin[1] = table(3, 6)
     own_into[...] = into[far]
     others = recv2.at[:, pl.ds(0, HALF - 1)]

time: 46.6 us -> 46.5 us (level)
  no operation moved by 1% of the time
where the time goes in v8:
time: 46.5 us; the launch traced here: 46.4 us
  Pallas kernels  45.8 us (98%)
  between operations  0.64 us (1%)
    pallas_call x1, Pallas kernels, shards(): pl.pallas_call(kernel, out_shape=(vmem(outs[0].shape, F32), vmem(outs[1]....  44.7 us
    pallas_call x1, Pallas kernels, shards(): pl.pallas_call(finish, out_shape=outs, in_specs=[inside] * 6, out_specs=(...  1.09 us

profile of v8, /device:TPU:1, one launch (start us, length us, event | category | flops | bytes accessed | tf_op | source)
XLA Modules:
  0.0 46.4 jit_solution(5138641662774347659)
XLA Ops:
  0.6 44.7 %shard_map.148 = (f32[2,8,64,128]{3,2,1,0:T(8,128)S(1)}, f32[2,64,128]{2,1,0:T(8,128)S(1)}, f32[128,128]{1,0:T(8,128)S(1)}, bf16[2,128,128]{2,1,0:T(8,128)(2,1)S...) custom-call(f32[8,32,64]{2,1,0:T(8,128)} %bitcast.2, f32[8]{0:T(128)} %step_hbm.1, f32[8]{0:T(128)} %pair_hbm.1, ...), custom_call_target="tpu_custom_call" | custom-call | tf_op jit(solution)/shard_map/pallas_call | solution.py:553
  45.3 1.1 %shard_map.149 = (f32[2,8,64,128]{3,2,1,0:T(8,128)}, f32[2,64,128]{2,1,0:T(8,128)}, f32[2,64,128]{2,1,0:T(8,128)}) custom-call(f32[2,8,64,128]{3,2,1,0:T(8,128)S(1)} %get-tuple-element.12.ext, f32[2,64,128]{2,1,0:T(8,128)S(1)} %get-tuple-element.13.val, f32[128,128]{1,0:T(8,128)S(1)} %get-tuple-element.14.arrived_rows, ...), custom_call_target="tpu_custom_call" | custom-call | tf_op jit(solution)/shard_map/pallas_call | solution.py:590

commit v9 on v8

--- a/solution.py
+++ b/solution.py
@@ -195,10 +195,6 @@
     lax.fori_loop(HALF, SEG - 1, greet_row, 0)
     lax.fori_loop(1, COLS, greet_col, 0)
 
-    @pl.when(far == 0)
-    def _():
-        lax.fori_loop(0, HALF, greet_row, 0)
-
 
     loads = [
         pltpu.make_async_copy(src, dst, load_sems.at[i])
@@ -236,7 +232,12 @@
     send1.reshape(LANES, LANES)[...] = head
     for c in range(2):
         recv1[c, slot] = send1[2 * group + c]
-    pl.semaphore_wait(barrier, HALF - 1 + COLS - 1 + HALF * far)
+    pl.semaphore_wait(barrier, HALF - 1 + COLS - 1 + far)
+
+    @pl.when(far == 0)
+    def _():
+        pl.semaphore_signal(barrier, inc=1, device_id={"row": me ^ 1}, device_id_type=MESH)
+
 
     def post1(k, to):
         peer = ring_step(k, me)

time: 46.5 us -> 46.5 us (level)
  no operation moved by 1% of the time
where the time goes in v9:
time: 46.5 us; the launch traced here: 46.4 us
  Pallas kernels  45.8 us (98%)
  between operations  0.64 us (1%)
    pallas_call x1, Pallas kernels, shards(): pl.pallas_call(kernel, out_shape=(vmem(outs[0].shape, F32), vmem(outs[1]....  44.7 us
    pallas_call x1, Pallas kernels, shards(): pl.pallas_call(finish, out_shape=outs, in_specs=[inside] * 6, out_specs=(...  1.09 us

profile of v9, /device:TPU:1, one launch (start us, length us, event | category | flops | bytes accessed | tf_op | source)
XLA Modules:
  0.0 46.4 jit_solution(1053342509596017064)
XLA Ops:
  0.6 44.7 %shard_map.148 = (f32[2,8,64,128]{3,2,1,0:T(8,128)S(1)}, f32[2,64,128]{2,1,0:T(8,128)S(1)}, f32[128,128]{1,0:T(8,128)S(1)}, bf16[2,128,128]{2,1,0:T(8,128)(2,1)S...) custom-call(f32[8,32,64]{2,1,0:T(8,128)} %bitcast.2, f32[8]{0:T(128)} %step_hbm.1, f32[8]{0:T(128)} %pair_hbm.1, ...), custom_call_target="tpu_custom_call" | custom-call | tf_op jit(solution)/shard_map/pallas_call | solution.py:554
  45.3 1.1 %shard_map.149 = (f32[2,8,64,128]{3,2,1,0:T(8,128)}, f32[2,64,128]{2,1,0:T(8,128)}, f32[2,64,128]{2,1,0:T(8,128)}) custom-call(f32[2,8,64,128]{3,2,1,0:T(8,128)S(1)} %get-tuple-element.12.ext, f32[2,64,128]{2,1,0:T(8,128)S(1)} %get-tuple-element.13.val, f32[128,128]{1,0:T(8,128)S(1)} %get-tuple-element.14.arrived_rows, ...), custom_call_target="tpu_custom_call" | custom-call | tf_op jit(solution)/shard_map/pallas_call | solution.py:591
